TPU v7x, 256 devices: a whole 4x4x8 slice. The times are simulated.
256 devices in a mesh: dp: 32 (over z_lo, x, y), tensor: 8 (over z_hi, core).
Axes of the slice: x: 4, y: 4, z: 8 (z_hi: 4, z_lo: 2; z = z_hi * 2 + z_lo), core: 2. Of those that a mesh axis runs over, the one named last changes fastest.
Arguments:
- activations: bfloat16 [8192, 14336], P('dp', 'tensor'), may hold values from -6 to 6
- out_grads: bfloat16 [8192, 4096], P('dp', 'tensor'), may hold values from -0.06591797 to 0.06591797
Outputs:
- fisher: float32 [14336, 4096], P('tensor', 'dp')
All inputs are finite; a program needn't handle non-finite values.
Results may differ from a plain program's by a relative error of at most 0.0003.
Values may be sent and summed in bfloat16 or wider, within the bound.
No kernel may reach another device: no remote copies, remote signals or barrier semaphores. Data moves between devices by JAX's collectives and lax.ppermute only.
A program may use at most 192 MiB of HBM per device.

v0:
```python
import jax
import jax.numpy as jnp
from jax import lax
from jax.sharding import PartitionSpec as P

LEN = 128


def per_device(activations, out_grads):
    gathered = lax.all_gather(out_grads, "tensor", axis=1, tiled=True)
    seq_count = activations.shape[0] // LEN
    features = activations.shape[1]
    inputs_seq = activations.reshape(seq_count, LEN, features)
    grads_seq = gathered.reshape(seq_count, LEN, gathered.shape[1])
    owned_cols = gathered.shape[1] // lax.axis_size("dp")

    def add_sequence(total, pair):
        grads = jnp.dot(pair[0].T, pair[1], preferred_element_type=jnp.float32)
        return (total + grads * grads, None)

    start_total = jnp.zeros((owned_cols * lax.axis_size("dp"), features), jnp.float32)
    total, unused = lax.scan(add_sequence, start_total, (grads_seq, inputs_seq))
    owned = lax.psum_scatter(total, "dp", scatter_dimension=0, tiled=True)
    return owned.T


def solution(mesh):
    in_specs = (P("dp", "tensor"), P("dp", "tensor"))
    out_specs = P("tensor", "dp")
    return jax.shard_map(
        per_device, mesh=mesh, in_specs=in_specs, out_specs=out_specs, check_vma=False
    )
```

profile of v0, /device:TPU:24, one launch (start us, length us, event | category | flops | bytes accessed | tf_op | source)
XLA Modules:
  0.0 434.8 jit_solution(9699238678097653621)
XLA Ops:
  6.5 0.0 all-gather.2.cloned.1.call-start
  6.5 0.7 all-gather.2.cloned.1.call-update
  7.3 0.0 reduce-scatter.2.cloned.1.call-start
  7.3 41.2 %all-gather.2.cloned.1.call-done = bf16[256,4096]{1,0:T(8,128)(2,1)} async-done(((bf16[256,512]{1,0:T(8,128)(2,1)}), bf16[256,4096]{1,0:T(8,128)(2,1)}) %all-gather.2.cloned.1.call-update) | async-done | bytes 2097168 | tf_op jit(solution)/shard_map/all_gather | solution.py:10
  48.5 33.2 %while.11 = (s32[]{:T(128)}, f32[4096,1792]{1,0:T(8,128)}, bf16[2,128,4096]{2,1,0:T(8,128)(2,1)}, bf16[2,128,1792]{2,1,0:T(8,128)(2,1)}, s32[]{:T(128)}, /*index=5*/s32[]{:T(128)}) while((s32[]{:T(128)}, f32[4096,1792]{1,0:T(8,128)}, bf16[2,128,4096]{2,1,0:T(8,128)(2,1)}, bf16[2,128,1792]{2,1,0:T(8,128)(2,1)}, s32[]{:T(128)}, ...), condition=%wide.region_1.2_spmd.clone, body=%wide.region_0.1_spmd.clone.sunk | while | flops 1901068288 | bytes 60229204 | solution.py:22
  48.5 12.8 %select_add_fusion.2 = f32[4096,1792]{1,0:T(8,128)} fusion(f32[4096,1792]{1,0:T(8,128)} %get-tuple-element.83, pred[]{:T(512)S(6)} %compare.3, bf16[2,128,4096]{2,1,0:T(8,128)(2,1)} %get-tuple-element.90, s32[]{:T(128)S(6)} %copy.6, bf16[2,128,1792]{2,1,0:T(8,128)(2,1)} %get-tuple-element.91), kind=kOutput, calls=%fused_computation.clone.1 | convolution fusion | flops 1901068288 | bytes 60229120 | tf_op jit(solution)/shard_map/while/body/eval_jaxpr/dot_general | solution.py:18
  61.3 20.4 %select_add_fusion.2 = f32[4096,1792]{1,0:T(8,128)} fusion(f32[4096,1792]{1,0:T(8,128)} %get-tuple-element.83, pred[]{:T(512)S(6)} %compare.3, bf16[2,128,4096]{2,1,0:T(8,128)(2,1)} %get-tuple-element.90, s32[]{:T(128)S(6)} %copy.6, bf16[2,128,1792]{2,1,0:T(8,128)(2,1)} %get-tuple-element.91), kind=kOutput, calls=%fused_computation.clone.1 | convolution fusion | flops 1901068288 | bytes 60229120 | tf_op jit(solution)/shard_map/while/body/eval_jaxpr/dot_general | solution.py:18
  81.7 29.5 %copy.3 = f32[4096,1792]{0,1:T(8,128)} copy(f32[4096,1792]{1,0:T(8,128)} %get-tuple-element.27) | data formatting | bytes 58720256 | tf_op jit(solution)/shard_map/while | solution.py:22
  111.2 0.0 reduce-scatter.2.cloned.1.call-update
  111.2 316.8 %reduce-scatter.2.cloned.1.call-done = f32[128,1792]{0,1:T(8,128)} async-done(((f32[4096,1792]{0,1:T(8,128)}), f32[128,1792]{0,1:T(8,128)}) %reduce-scatter.2.cloned.1.call-update) | async-done | bytes 917520 | tf_op jit(solution)/shard_map/reduce_scatter | solution.py:23
  (1 shorter events, 0.0 us)
Async XLA Ops:
  6.5 41.9 %all-gather.2.cloned.1.call-start = ((), (), s32[]{:S(2)}) async-start(), calls=%async_computation.1 | async-start | bytes 2359296 | tf_op jit(solution)/shard_map/all_gather | solution.py:10
  7.3 420.7 %reduce-scatter.2.cloned.1.call-start = ((), (), s32[]{:S(2)}) async-start(), calls=%async_computation.2 | async-start | bytes 30277632 | tf_op jit(solution)/shard_map/reduce_scatter | solution.py:23
Sparse Core Ops, SparseCore 0:
  9.2 39.2 all-gather.1
  111.4 316.5 reduce-scatter.1
where the time goes:
time: 441 us; the launch traced here: 435 us
  waiting for transfers between devices  359 us (81%)
  matrix products  33.2 us (8%)
  local copies, waits for them, and re-layouts  29.5 us (7%)
  between operations  13.4 us (3%)
    reduce_scatter x1, waiting for transfers between devices, per_device(): owned = lax.psum_scatter(total, 'dp', scatter_dimension=0, tiled=True)  317 us
    all_gather x1, waiting for transfers between devices, per_device(): gathered = lax.all_gather(out_grads, 'tensor', axis=1, tiled=True)  41.2 us
    dot_general x2, matrix products, add_sequence(): grads = jnp.dot(pair[0].T, pair[1], preferred_element_type=jnp.float32)  33.2 us
    while x1, local copies, waits for them, and re-layouts, per_device(): total, unused = lax.scan(add_sequence, start_total, (grads_seq, inputs_seq))  29.5 us
  transfers between devices with their start and end apart: 2, of which 2 were waited for; matrix products, arithmetic and copies ran while one was open for 0% of the time, Pallas kernels for 0%

commit v1 on v0

v1 whole, which is shorter than its diff:
```python
import functools

import jax
import jax.numpy as jnp
from jax import lax
from jax.experimental import pallas as pl
from jax.experimental.pallas import tpu as pltpu
from jax.sharding import PartitionSpec as P

LEN = 128
NX, NY, NZ = 4, 4, 4
TILE = 256
CHUNKS = (768, 512, 512)
CODE_TOP = 2.0**14
LEAST = 2.0**-120
VMEM = 48 * 1024 * 1024


def dp_index(z, x, y):
    return (z % 2) * NX * NY + (x % NX) * NY + (y % NY)


def dp_moves(dz, dx, dy):
    return [
        (dp_index(z, x, y), dp_index(z + dz, x + dx, y + dy))
        for z in range(2)
        for x in range(NX)
        for y in range(NY)
    ]


def tensor_moves(dz, flip):
    return [
        (2 * z + c, 2 * ((z + dz) % NZ) + (c ^ flip))
        for z in range(NZ)
        for c in range(2)
    ]


def from_y(array, offset):
    return lax.ppermute(array, "dp", dp_moves(0, 0, -offset))


def to_x(array, offset):
    return lax.ppermute(array, "dp", dp_moves(0, offset, 0))


def to_z_lo(array):
    return lax.ppermute(array, "dp", dp_moves(1, 0, 0))


def from_z(array, offset):
    return lax.ppermute(array, "tensor", tensor_moves(-offset, 0))


def from_core(array):
    return lax.ppermute(array, "tensor", tensor_moves(0, 1))


def encode(total):
    top = jnp.max(total, axis=0, keepdims=True)
    top = jnp.maximum(top, LEAST).astype(jnp.bfloat16).astype(jnp.float32)
    scaled = total * (1.0 / top) * CODE_TOP
    scaled = scaled * scaled
    scaled = scaled * scaled
    scaled = scaled * scaled
    return scaled.astype(jnp.bfloat16), top


def decode(code, top):
    value = jnp.maximum(code.astype(jnp.float32), 2.0**-126)
    return jnp.exp(jnp.log(value) * 0.125) * (top * (1.0 / CODE_TOP))


def put_one(ref, total):
    code, top = encode(total)
    ref[:LEN, :] = code
    ref[LEN:, :] = jnp.broadcast_to(top, (16, top.shape[1])).astype(jnp.bfloat16)


def put_two(ref, first, second):
    code_0, top_0 = encode(first)
    code_1, top_1 = encode(second)
    ref[:LEN, :] = code_0
    ref[LEN : 2 * LEN, :] = code_1
    shape = (8, top_0.shape[1])
    tops = jnp.concatenate(
        [jnp.broadcast_to(top_0, shape), jnp.broadcast_to(top_1, shape)], axis=0
    )
    ref[2 * LEN :, :] = tops.astype(jnp.bfloat16)


def get_one(ref):
    tops = ref[LEN:, :].astype(jnp.float32)
    return decode(ref[:LEN, :], tops[:1])


def get_two(ref, which):
    tops = ref[2 * LEN :, :].astype(jnp.float32)
    return decode(ref[which * LEN : (which + 1) * LEN, :], tops[8 * which : 8 * which + 1])


def partial_kernel(
    slots, a_0, a_1, a_2a, a_2b, a_3, grads, own, keep_up, keep_down, up, down
):
    def total_of(k, j):
        block = slots[4 * j + k]
        total = None
        for o, pair in enumerate(
            (
                (a_0[:LEN, :], a_0[LEN:, :]),
                (a_1[:LEN, :], a_1[LEN:, :]),
                (a_2a[...], a_2b[...]),
                (a_3[:LEN, :], a_3[LEN:, :]),
            )
        ):
            for s in range(2):
                found = jnp.dot(
                    grads[block, o, :, s * LEN : (s + 1) * LEN],
                    pair[s],
                    preferred_element_type=jnp.float32,
                )
                total = found * found if total is None else total + found * found
        return total

    put_two(up, total_of(2, 0), total_of(1, 1))
    put_two(down, total_of(2, 1), total_of(3, 0))
    keep_up[...] = total_of(1, 0)
    keep_down[...] = total_of(3, 1)
    own[:LEN, :] = total_of(0, 0)
    own[LEN:, :] = total_of(0, 1)


def call(body, name, features, tall_in, tall_out, flops):
    in_bytes = sum(h * features * (2 if t == jnp.bfloat16 else 4) for h, t in tall_in)
    out_bytes = sum(h * features * (2 if t == jnp.bfloat16 else 4) for h, t in tall_out)
    return pl.pallas_call(
        body,
        name=name,
        grid=(features // TILE,),
        in_specs=[pl.BlockSpec((h, TILE), lambda i: (0, i)) for h, _ in tall_in],
        out_specs=[pl.BlockSpec((h, TILE), lambda i: (0, i)) for h, _ in tall_out],
        out_shape=[jax.ShapeDtypeStruct((h, features), t) for h, t in tall_out],
        compiler_params=pltpu.CompilerParams(vmem_limit_bytes=VMEM),
        cost_estimate=pl.CostEstimate(
            flops=flops, bytes_accessed=in_bytes + out_bytes, transcendentals=0
        ),
    )


def partial_sums(slots, acts, grads):
    features = acts[0].shape[1]
    f32, b16 = jnp.float32, jnp.bfloat16
    outs = ((2 * LEN, f32), (LEN, f32), (LEN, f32), (2 * LEN + 16, b16), (2 * LEN + 16, b16))
    return pl.pallas_call(
        partial_kernel,
        name="partial_sums",
        grid_spec=pltpu.PrefetchScalarGridSpec(
            num_scalar_prefetch=1,
            grid=(features // TILE,),
            in_specs=[
                pl.BlockSpec((a.shape[0], TILE), lambda i, s: (0, i)) for a in acts
            ]
            + [pl.BlockSpec(grads.shape, lambda i, s: (0, 0, 0, 0))],
            out_specs=[pl.BlockSpec((h, TILE), lambda i, s: (0, i)) for h, _ in outs],
        ),
        out_shape=[jax.ShapeDtypeStruct((h, features), t) for h, t in outs],
        compiler_params=pltpu.CompilerParams(vmem_limit_bytes=VMEM),
        cost_estimate=pl.CostEstimate(
            flops=2 * 1024 * 1024 * features, bytes_accessed=2**21, transcendentals=0
        ),
    )(slots, *acts, grads)


def relay_kernel(keep_up, keep_down, from_down, from_up, up, down):
    put_one(up, keep_up[...] + get_two(from_down, 0))
    put_one(down, keep_down[...] + get_two(from_up, 0))


def gather_kernel(own, from_down, from_up, late_down, late_up, kept, sent):
    kept[...] = own[:LEN, :] + (get_two(from_up, 1) + get_one(late_down))
    put_one(sent, own[LEN:, :] + (get_two(from_down, 1) + get_one(late_up)))


def final_kernel(kept, received, out):
    out[...] = (kept[...] + get_one(received)).T


def final(kept, received):
    features = kept.shape[1]
    return pl.pallas_call(
        final_kernel,
        name="final",
        grid=(features // TILE,),
        in_specs=[
            pl.BlockSpec((LEN, TILE), lambda i: (0, i)),
            pl.BlockSpec((LEN + 16, TILE), lambda i: (0, i)),
        ],
        out_specs=pl.BlockSpec((TILE, LEN), lambda i: (i, 0)),
        out_shape=jax.ShapeDtypeStruct((features, LEN), jnp.float32),
        compiler_params=pltpu.CompilerParams(vmem_limit_bytes=VMEM),
    )(kept, received)


def gather_grads(out_grads, y):
    turned = out_grads.T
    width = turned.shape[0] // NY

    def block_for(offset):
        start = ((y + offset) % NY) * width
        return lax.dynamic_slice_in_dim(turned, start, width, axis=0)

    mine = jnp.stack(
        [block_for(0)] + [from_y(block_for(-o), o) for o in range(1, NY)]
    )
    z_up = from_z(mine, 1)
    z_down = from_z(mine, -1)
    far = jnp.concatenate([from_z(z_down[:2], -1), from_z(z_up[2:], 1)])
    near = jnp.stack([z_up, z_down])
    other_mine = from_core(mine)
    other_near = from_core(near)
    other_far = from_core(far)
    return jnp.stack(
        [mine, other_mine, z_up, other_near[0], far, other_far, z_down, other_near[1]]
    )


def gather_acts(chunk):
    after = from_y(chunk, 1)
    before = from_y(chunk, -1)
    far_a = from_y(before[:LEN], -1)
    far_b = from_y(after[LEN:], 1)
    return chunk, after, far_a, far_b, before


def per_device(activations, out_grads):
    f32, b16 = jnp.float32, jnp.bfloat16
    dp, tensor = lax.axis_index("dp"), lax.axis_index("tensor")
    z_lo, x, y = dp // (NX * NY), (dp // NY) % NX, dp % NY
    z_hi, core = tensor // 2, tensor % 2
    slots = []
    for j in range(2):
        for k in range(NX):
            wanted = ((z_lo + j) % 2) * NX + (x + k) % NX
            slots.append(((wanted // 2 - z_hi) % NZ) * 2 + (wanted + core) % 2)
    slots = jnp.stack(slots).astype(jnp.int32)

    grads = gather_grads(out_grads, y)
    starts = [sum(CHUNKS[:i]) for i in range(len(CHUNKS))]
    results = []
    for start, size in zip(starts, CHUNKS, strict=True):
        acts = gather_acts(activations[:, start : start + size])
        own, keep_up, keep_down, up, down = partial_sums(slots, acts, grads)
        from_down, from_up = to_x(up, 1), to_x(down, -1)
        one, two = LEN + 16, 2 * LEN + 16
        up, down = call(
            relay_kernel,
            "relay",
            size,
            ((LEN, f32), (LEN, f32), (two, b16), (two, b16)),
            ((one, b16), (one, b16)),
            16 * LEN * size,
        )(keep_up, keep_down, from_down, from_up)
        late_down, late_up = to_x(up, 1), to_x(down, -1)
        kept, sent = call(
            gather_kernel,
            "gather",
            size,
            ((2 * LEN, f32), (two, b16), (two, b16), (one, b16), (one, b16)),
            ((LEN, f32), (one, b16)),
            32 * LEN * size,
        )(own, from_down, from_up, late_down, late_up)
        results.append(final(kept, to_z_lo(sent)))
    return jnp.concatenate(results)


def solution(mesh):
    in_specs = (P("dp", "tensor"), P("dp", "tensor"))
    out_specs = P("tensor", "dp")
    return jax.shard_map(
        per_device, mesh=mesh, in_specs=in_specs, out_specs=out_specs, check_vma=False
    )
```

time: 441 us -> 108 us (0.24); the launches traced: 435 us -> 107 us
  waiting for transfers between devices: 359 us -> 33.5 us
  starting transfers between devices: 0.04 us -> 51.5 us
  matrix products: 33.2 us -> 0 us
  local copies, waits for them, and re-layouts: 29.5 us -> 2.86 us
  Pallas kernels: 0 us -> 16.2 us
  between operations: 13.4 us -> 0.97 us
    reduce_scatter x1 -> x0, waiting for transfers between devices: 317 us -> none  [per_device(): owned = lax.psum_scatter(total, 'dp', scatter_dimension=0, tiled=True)]
    ppermute x0 -> x37, starting transfers between devices: none -> 51.5 us  [the longest x15 20.2 us: from_y(): return lax.ppermute(array, 'dp', dp_moves(0, 0, -offset))]
    all_gather x1 -> x0, waiting for transfers between devices: 41.2 us -> none  [per_device(): gathered = lax.all_gather(out_grads, 'tensor', axis=1, tiled=True)]
    ppermute x0 -> x37, waiting for transfers between devices: none -> 33.5 us  [the longest x4 15.6 us: from_z(): return lax.ppermute(array, 'tensor', tensor_moves(-offset, 0))]
    dot_general x2 -> x0, matrix products: 33.2 us -> none  [add_sequence(): grads = jnp.dot(pair[0].T, pair[1], preferred_element_type=jnp.float32)]
    while x1 -> x0, local copies, waits for them, and re-layouts: 29.5 us -> none  [per_device(): total, unused = lax.scan(add_sequence, start_total, (grads_seq, inputs_seq))]
    pallas_call x0 -> x12, Pallas kernels: none -> 16.2 us  [the longest x3 11.4 us: partial_sums(): pl.pallas_call(partial_kernel, name='partial_sums', grid_spec=pltpu.Prefe...]
  transfers between devices with their start and end apart: 2 -> 37, of which waited for: 2 -> 12; matrix products, arithmetic and copies ran while one was open for 0% -> 3% of each run, Pallas kernels for 0% -> 15%
where the time goes in v1:
time: 108 us; the launch traced here: 107 us
  starting transfers between devices  51.5 us (48%)
  waiting for transfers between devices  33.5 us (31%)
  Pallas kernels  16.2 us (15%)
  local copies, waits for them, and re-layouts  2.86 us (3%)
  other arithmetic  1.96 us (2%)
    ppermute x15, starting transfers between devices, from_y(): return lax.ppermute(array, 'dp', dp_moves(0, 0, -offset))  20.2 us
    ppermute x12, starting transfers between devices, to_x(): return lax.ppermute(array, 'dp', dp_moves(0, offset, 0))  16.2 us
    ppermute x4, waiting for transfers between devices, from_z(): return lax.ppermute(array, 'tensor', tensor_moves(-offset, 0))  15.6 us
    pallas_call x3, Pallas kernels, partial_sums(): pl.pallas_call(partial_kernel, name='partial_sums', grid_spec=pltpu.Prefe...  11.4 us
    ppermute x4, starting transfers between devices, from_z(): return lax.ppermute(array, 'tensor', tensor_moves(-offset, 0))  9.53 us
    ppermute x15, waiting for transfers between devices, from_y(): return lax.ppermute(array, 'dp', dp_moves(0, 0, -offset))  7.85 us
    ppermute x3, starting transfers between devices, to_z_lo(): return lax.ppermute(array, 'dp', dp_moves(1, 0, 0))  5.19 us
    ppermute x12, waiting for transfers between devices, to_x(): return lax.ppermute(array, 'dp', dp_moves(0, offset, 0))  4.9 us
  transfers between devices with their start and end apart: 37, of which 12 were waited for; matrix products, arithmetic and copies ran while one was open for 3% of the time, Pallas kernels for 15%

profile of v1, /device:TPU:24, one launch (start us, length us, event | category | flops | bytes accessed | tf_op | source)
XLA Modules:
  0.0 106.9 jit_solution(13911488299311706602)
XLA Ops:
  2.1 2.8 %collective-permute-start.5 = (bf16[128,256]{1,0:T(8,128)(2,1)S(1)}, bf16[128,256]{1,0:T(8,128)(2,1)S(1)}, u32[]{:S(2)}, u32[]{:S(2)}) collective-permute-start(bf16[128,256]{1,0:T(8,128)(2,1)S(1)} %bitcast.40), channel_id=1, source_target_pairs={{0,16},{8,24},{16,0},{24,8},{32,48},{40,56},{48,32},{56,40},{64,80... | collective-permute-start | bytes 196616 | tf_op jit(solution)/shard_map/ppermute | solution.py:41
  10.0 5.2 %collective-permute-start.8 = (bf16[4,128,256]{2,1,0:T(8,128)(2,1)S(1)}, bf16[4,128,256]{2,1,0:T(8,128)(2,1)S(1)}, u32[]{:S(2)}, u32[]{:S(2)}) collective-permute-start(bf16[4,128,256]{2,1,0:T(8,128)(2,1)S(1)} %pad_maximum_fusion.2), channel_id=1, source_target_pairs={{0,6},{1,7},{2,0},{3,1},{4,2},{5,3},{6,4},{7,5},{8,14},{9,15},{10,... | collective-permute-start | bytes 786440 | tf_op jit(solution)/shard_map/ppermute | solution.py:53
  16.9 8.1 %collective-permute-done.8 = bf16[4,128,256]{2,1,0:T(8,128)(2,1)S(1)} collective-permute-done((bf16[4,128,256]{2,1,0:T(8,128)(2,1)S(1)}, bf16[4,128,256]{2,1,0:T(8,128)(2,1)S(1)}, u32[]{:S(2)}, u32[]{:S(2)}) %collective-permute-start.8) | collective-permute-done | bytes 262176 | tf_op jit(solution)/shard_map/ppermute | solution.py:53
  25.0 3.8 %collective-permute-done.9 = bf16[4,128,256]{2,1,0:T(8,128)(2,1)S(1)} collective-permute-done((bf16[4,128,256]{2,1,0:T(8,128)(2,1)S(1)}, bf16[4,128,256]{2,1,0:T(8,128)(2,1)S(1)}, u32[]{:S(2)}, u32[]{:S(2)}) %collective-permute-start.9) | collective-permute-done | bytes 262176 | tf_op jit(solution)/shard_map/ppermute | solution.py:53
  29.2 4.2 %collective-permute-start.12 = (bf16[2,128,256]{2,1,0:T(8,128)(2,1)S(1)}, bf16[2,128,256]{2,1,0:T(8,128)(2,1)S(1)}, u32[]{:S(2)}, u32[]{:S(2)}) collective-permute-start(bf16[2,128,256]{2,1,0:T(8,128)(2,1)S(1)} %slice.56), channel_id=1, source_target_pairs={{0,6},{1,7},{2,0},{3,1},{4,2},{5,3},{6,4},{7,5},{8,14},{9,15},{10,... | collective-permute-start | bytes 393224 | tf_op jit(solution)/shard_map/ppermute | solution.py:53
  33.4 2.4 %collective-permute-start.20 = (bf16[256,512]{1,0:T(8,128)(2,1)S(1)}, bf16[256,512]{1,0:T(8,128)(2,1)S(1)}, u32[]{:S(2)}, u32[]{:S(2)}) collective-permute-start(bf16[256,512]{1,0:T(8,128)(2,1)S(1)} %get-tuple-element.59.a_0), channel_id=1, source_target_pairs={{0,8},{8,16},{16,24},{24,0},{32,40},{40,48},{48,56},{56,32},{64,72... | collective-permute-start | bytes 786440 | tf_op jit(solution)/shard_map/ppermute | solution.py:41
  36.0 3.7 %collective-permute-done.11 = bf16[2,128,256]{2,1,0:T(8,128)(2,1)S(1)} collective-permute-done((bf16[2,128,256]{2,1,0:T(8,128)(2,1)S(1)}, bf16[2,128,256]{2,1,0:T(8,128)(2,1)S(1)}, u32[]{:S(2)}, u32[]{:S(2)}) %collective-permute-start.11) | collective-permute-done | bytes 131104 | tf_op jit(solution)/shard_map/ppermute | solution.py:53
  39.6 2.3 %collective-permute-start.29 = (bf16[256,512]{1,0:T(8,128)(2,1)S(1)}, bf16[256,512]{1,0:T(8,128)(2,1)S(1)}, u32[]{:S(2)}, u32[]{:S(2)}) collective-permute-start(bf16[256,512]{1,0:T(8,128)(2,1)S(1)} %get-tuple-element.60.a_0), channel_id=1, source_target_pairs={{0,8},{8,16},{16,24},{24,0},{32,40},{40,48},{48,56},{56,32},{64,72... | collective-permute-start | bytes 786440 | tf_op jit(solution)/shard_map/ppermute | solution.py:41
  46.0 5.7 %collective-permute-done.2.a_2a = bf16[128,768]{1,0:T(8,128)(2,1)S(1)} collective-permute-done((bf16[128,768]{1,0:T(8,128)(2,1)S(1)}, bf16[128,768]{1,0:T(8,128)(2,1)S(1)}, u32[]{:S(2)}, u32[]{:S(2)}) %collective-permute-start.2) | collective-permute-done | bytes 196640 | tf_op jit(solution)/shard_map/ppermute | solution.py:41
  53.2 4.7 %partial_sums.3 = (f32[256,768]{1,0:T(8,128)S(1)}, f32[128,768]{1,0:T(8,128)S(1)}, f32[128,768]{1,0:T(8,128)S(1)}, bf16[272,768]{1,0:T(8,128)(2,1)S(1)}, bf16[272,768]{1,0:T(8,128)(2,1)S(1)}) custom-call(s32[8]{0:T(128)S(1)} %stack.76.slots, bf16[256,768]{1,0:T(8,128)(2,1)S(1)} %slice.39.a_0, bf16[256,768]{1,0:T(8,128)(2,1)S(1)} %collective-permute-done.a_1, ...), custom_call_target="tpu_custom_call" | custom-call | flops 1610612736 | bytes 2097152 | tf_op jit(solution)/shard_map/partial_sums/pallas_call | solution.py:155
  59.5 2.0 %collective-permute-start.21 = (bf16[128,512]{1,0:T(8,128)(2,1)S(1)}, bf16[128,512]{1,0:T(8,128)(2,1)S(1)}, u32[]{:S(2)}, u32[]{:S(2)}) collective-permute-start(bf16[128,512]{1,0:T(8,128)(2,1)S(1)} %slice.58), channel_id=1, source_target_pairs={{0,8},{8,16},{16,24},{24,0},{32,40},{40,48},{48,56},{56,32},{64,72... | collective-permute-start | bytes 393224 | tf_op jit(solution)/shard_map/ppermute | solution.py:41
  61.7 1.8 %collective-permute-start.15 = (bf16[272,768]{1,0:T(8,128)(2,1)S(1)}, bf16[272,768]{1,0:T(8,128)(2,1)S(1)}, u32[]{:S(2)}, u32[]{:S(2)}) collective-permute-start(bf16[272,768]{1,0:T(8,128)(2,1)S(1)} %get-tuple-element.34), channel_id=1, source_target_pairs={{0,96},{8,104},{16,112},{24,120},{32,0},{40,8},{48,16},{56,24},{64... | collective-permute-start | bytes 1253384 | tf_op jit(solution)/shard_map/ppermute | solution.py:45
  63.5 3.2 %collective-permute-start.30 = (bf16[128,512]{1,0:T(8,128)(2,1)S(1)}, bf16[128,512]{1,0:T(8,128)(2,1)S(1)}, u32[]{:S(2)}, u32[]{:S(2)}) collective-permute-start(bf16[128,512]{1,0:T(8,128)(2,1)S(1)} %slice.60), channel_id=1, source_target_pairs={{0,8},{8,16},{16,24},{24,0},{32,40},{40,48},{48,56},{56,32},{64,72... | collective-permute-start | bytes 393224 | tf_op jit(solution)/shard_map/ppermute | solution.py:41
  67.8 3.3 %partial_sums.4 = (f32[256,512]{1,0:T(8,128)S(1)}, f32[128,512]{1,0:T(8,128)S(1)}, f32[128,512]{1,0:T(8,128)S(1)}, bf16[272,512]{1,0:T(8,128)(2,1)S(1)}, bf16[272,512]{1,0:T(8,128)(2,1)S(1)}) custom-call(s32[8]{0:T(128)S(1)} %stack.76.slots, bf16[256,512]{1,0:T(8,128)(2,1)S(1)} %get-tuple-element.59.a_0, bf16[256,512]{1,0:T(8,128)(2,1)S(1)} %collective-permute-done.19.a_1, ...), custom_call_target="tpu_custom_call" | custom-call | flops 1073741824 | bytes 2097152 | tf_op jit(solution)/shard_map/partial_sums/pallas_call | solution.py:155
  71.2 2.7 %collective-permute-start.23 = (bf16[272,512]{1,0:T(8,128)(2,1)S(1)}, bf16[272,512]{1,0:T(8,128)(2,1)S(1)}, u32[]{:S(2)}, u32[]{:S(2)}) collective-permute-start(bf16[272,512]{1,0:T(8,128)(2,1)S(1)} %get-tuple-element.42), channel_id=1, source_target_pairs={{0,32},{8,40},{16,48},{24,56},{32,64},{40,72},{48,80},{56,88},{64,... | collective-permute-start | bytes 835592 | tf_op jit(solution)/shard_map/ppermute | solution.py:45
  74.5 3.3 %partial_sums.5 = (f32[256,512]{1,0:T(8,128)S(1)}, f32[128,512]{1,0:T(8,128)S(1)}, f32[128,512]{1,0:T(8,128)S(1)}, bf16[272,512]{1,0:T(8,128)(2,1)S(1)}, bf16[272,512]{1,0:T(8,128)(2,1)S(1)}) custom-call(s32[8]{0:T(128)S(1)} %stack.76.slots, bf16[256,512]{1,0:T(8,128)(2,1)S(1)} %get-tuple-element.60.a_0, bf16[256,512]{1,0:T(8,128)(2,1)S(1)} %collective-permute-done.28.a_1, ...), custom_call_target="tpu_custom_call" | custom-call | flops 1073741824 | bytes 2097152 | tf_op jit(solution)/shard_map/partial_sums/pallas_call | solution.py:155
  77.8 1.7 %collective-permute-start.32 = (bf16[272,512]{1,0:T(8,128)(2,1)S(1)}, bf16[272,512]{1,0:T(8,128)(2,1)S(1)}, u32[]{:S(2)}, u32[]{:S(2)}) collective-permute-start(bf16[272,512]{1,0:T(8,128)(2,1)S(1)} %get-tuple-element.51), channel_id=1, source_target_pairs={{0,32},{8,40},{16,48},{24,56},{32,64},{40,72},{48,80},{56,88},{64,... | collective-permute-start | bytes 835592 | tf_op jit(solution)/shard_map/ppermute | solution.py:45
  79.5 1.9 %collective-permute-start.33 = (bf16[272,512]{1,0:T(8,128)(2,1)S(1)}, bf16[272,512]{1,0:T(8,128)(2,1)S(1)}, u32[]{:S(2)}, u32[]{:S(2)}) collective-permute-start(bf16[272,512]{1,0:T(8,128)(2,1)S(1)} %get-tuple-element.52), channel_id=1, source_target_pairs={{0,96},{8,104},{16,112},{24,120},{32,0},{40,8},{48,16},{56,24},{64... | collective-permute-start | bytes 835592 | tf_op jit(solution)/shard_map/ppermute | solution.py:45
  82.3 3.1 %collective-permute-start.17 = (bf16[144,768]{1,0:T(8,128)(2,1)S(1)}, bf16[144,768]{1,0:T(8,128)(2,1)S(1)}, u32[]{:S(2)}, u32[]{:S(2)}) collective-permute-start(bf16[144,768]{1,0:T(8,128)(2,1)S(1)} %get-tuple-element.38), channel_id=1, source_target_pairs={{0,96},{8,104},{16,112},{24,120},{32,0},{40,8},{48,16},{56,24},{64... | collective-permute-start | bytes 663560 | tf_op jit(solution)/shard_map/ppermute | solution.py:45
  86.0 2.9 %collective-permute-done.32.from_down = bf16[272,512]{1,0:T(8,128)(2,1)S(1)} collective-permute-done((bf16[272,512]{1,0:T(8,128)(2,1)S(1)}, bf16[272,512]{1,0:T(8,128)(2,1)S(1)}, u32[]{:S(2)}, u32[]{:S(2)}) %collective-permute-start.32) | collective-permute-done | bytes 278560 | tf_op jit(solution)/shard_map/ppermute | solution.py:45
  89.7 1.8 %collective-permute-start.34 = (bf16[144,512]{1,0:T(8,128)(2,1)S(1)}, bf16[144,512]{1,0:T(8,128)(2,1)S(1)}, u32[]{:S(2)}, u32[]{:S(2)}) collective-permute-start(bf16[144,512]{1,0:T(8,128)(2,1)S(1)} %get-tuple-element.55), channel_id=1, source_target_pairs={{0,32},{8,40},{16,48},{24,56},{32,64},{40,72},{48,80},{56,88},{64,... | collective-permute-start | bytes 442376 | tf_op jit(solution)/shard_map/ppermute | solution.py:45
  94.8 1.7 %collective-permute-start.18 = (bf16[144,768]{1,0:T(8,128)(2,1)S(1)}, bf16[144,768]{1,0:T(8,128)(2,1)S(1)}, u32[]{:S(2)}, u32[]{:S(2)}) collective-permute-start(bf16[144,768]{1,0:T(8,128)(2,1)S(1)} %get-tuple-element.40), channel_id=1, source_target_pairs={{0,128},{8,136},{16,144},{24,152},{32,160},{40,168},{48,176},{56,1... | collective-permute-start | bytes 663560 | tf_op jit(solution)/shard_map/ppermute | solution.py:49
  98.8 2.4 %collective-permute-start.36 = (bf16[144,512]{1,0:T(8,128)(2,1)S(1)}, bf16[144,512]{1,0:T(8,128)(2,1)S(1)}, u32[]{:S(2)}, u32[]{:S(2)}) collective-permute-start(bf16[144,512]{1,0:T(8,128)(2,1)S(1)} %get-tuple-element.58), channel_id=1, source_target_pairs={{0,128},{8,136},{16,144},{24,152},{32,160},{40,168},{48,176},{56,1... | collective-permute-start | bytes 442376 | tf_op jit(solution)/shard_map/ppermute | solution.py:49
  101.2 2.4 %collective-permute-done.27.received = bf16[144,512]{1,0:T(8,128)(2,1)S(1)} collective-permute-done((bf16[144,512]{1,0:T(8,128)(2,1)S(1)}, bf16[144,512]{1,0:T(8,128)(2,1)S(1)}, u32[]{:S(2)}, u32[]{:S(2)}) %collective-permute-start.27) | collective-permute-done | bytes 147488 | tf_op jit(solution)/shard_map/ppermute | solution.py:49
  (97 shorter events, 29.0 us)
Async XLA Ops:
  6.5 26.9 %collective-permute-start.1 = (bf16[256,768]{1,0:T(8,128)(2,1)S(1)}, bf16[256,768]{1,0:T(8,128)(2,1)S(1)}, u32[]{:S(2)}, u32[]{:S(2)}) collective-permute-start(bf16[256,768]{1,0:T(8,128)(2,1)S(1)} %slice.39.a_0), channel_id=1, source_target_pairs={{0,8},{8,16},{16,24},{24,0},{32,40},{40,48},{48,56},{56,32},{64,72... | collective-permute-start | bytes 1179656 | tf_op jit(solution)/shard_map/ppermute | solution.py:41
  7.6 28.3 %collective-permute-start = (bf16[256,768]{1,0:T(8,128)(2,1)S(1)}, bf16[256,768]{1,0:T(8,128)(2,1)S(1)}, u32[]{:S(2)}, u32[]{:S(2)}) collective-permute-start(bf16[256,768]{1,0:T(8,128)(2,1)S(1)} %slice.39.a_0), channel_id=1, source_target_pairs={{0,24},{8,0},{16,8},{24,16},{32,56},{40,32},{48,40},{56,48},{64,88... | collective-permute-start | bytes 1179656 | tf_op jit(solution)/shard_map/ppermute | solution.py:41
  10.0 15.1 %collective-permute-start.8 = (bf16[4,128,256]{2,1,0:T(8,128)(2,1)S(1)}, bf16[4,128,256]{2,1,0:T(8,128)(2,1)S(1)}, u32[]{:S(2)}, u32[]{:S(2)}) collective-permute-start(bf16[4,128,256]{2,1,0:T(8,128)(2,1)S(1)} %pad_maximum_fusion.2), channel_id=1, source_target_pairs={{0,6},{1,7},{2,0},{3,1},{4,2},{5,3},{6,4},{7,5},{8,14},{9,15},{10,... | collective-permute-start | bytes 786440 | tf_op jit(solution)/shard_map/ppermute | solution.py:53
  15.2 13.6 %collective-permute-start.9 = (bf16[4,128,256]{2,1,0:T(8,128)(2,1)S(1)}, bf16[4,128,256]{2,1,0:T(8,128)(2,1)S(1)}, u32[]{:S(2)}, u32[]{:S(2)}) collective-permute-start(bf16[4,128,256]{2,1,0:T(8,128)(2,1)S(1)} %pad_maximum_fusion.2), channel_id=1, source_target_pairs={{0,2},{1,3},{2,4},{3,5},{4,6},{5,7},{6,0},{7,1},{8,10},{9,11},{10,... | collective-permute-start | bytes 786440 | tf_op jit(solution)/shard_map/ppermute | solution.py:53
  15.3 13.9 %collective-permute-start.7 = (bf16[4,128,256]{2,1,0:T(8,128)(2,1)S(1)}, bf16[4,128,256]{2,1,0:T(8,128)(2,1)S(1)}, u32[]{:S(2)}, u32[]{:S(2)}) collective-permute-start(bf16[4,128,256]{2,1,0:T(8,128)(2,1)S(1)} %pad_maximum_fusion.2), channel_id=1, source_target_pairs={{0,1},{1,0},{2,3},{3,2},{4,5},{5,4},{6,7},{7,6},{8,9},{9,8},{10,11... | collective-permute-start | bytes 786440 | tf_op jit(solution)/shard_map/ppermute | solution.py:57
  28.9 13.7 %collective-permute-start.10 = (bf16[2,4,128,256]{3,2,1,0:T(8,128)(2,1)S(1)}, bf16[2,4,128,256]{3,2,1,0:T(8,128)(2,1)S(1)}, u32[]{:S(2)}, u32[]{:S(2)}) collective-permute-start(bf16[2,4,128,256]{3,2,1,0:T(8,128)(2,1)S(1)} %pad_maximum_fusion.1), channel_id=1, source_target_pairs={{0,1},{1,0},{2,3},{3,2},{4,5},{5,4},{6,7},{7,6},{8,9},{9,8},{10,11... | collective-permute-start | bytes 1572872 | tf_op jit(solution)/shard_map/ppermute | solution.py:57
  29.0 10.6 %collective-permute-start.11 = (bf16[2,128,256]{2,1,0:T(8,128)(2,1)S(1)}, bf16[2,128,256]{2,1,0:T(8,128)(2,1)S(1)}, u32[]{:S(2)}, u32[]{:S(2)}) collective-permute-start(bf16[2,128,256]{2,1,0:T(8,128)(2,1)S(1)} %slice.55), channel_id=1, source_target_pairs={{0,2},{1,3},{2,4},{3,5},{4,6},{5,7},{6,0},{7,1},{8,10},{9,11},{10,... | collective-permute-start | bytes 393224 | tf_op jit(solution)/shard_map/ppermute | solution.py:53
  29.2 12.8 %collective-permute-start.12 = (bf16[2,128,256]{2,1,0:T(8,128)(2,1)S(1)}, bf16[2,128,256]{2,1,0:T(8,128)(2,1)S(1)}, u32[]{:S(2)}, u32[]{:S(2)}) collective-permute-start(bf16[2,128,256]{2,1,0:T(8,128)(2,1)S(1)} %slice.56), channel_id=1, source_target_pairs={{0,6},{1,7},{2,0},{3,1},{4,2},{5,3},{6,4},{7,5},{8,14},{9,15},{10,... | collective-permute-start | bytes 393224 | tf_op jit(solution)/shard_map/ppermute | solution.py:53
  33.4 26.1 %collective-permute-start.20 = (bf16[256,512]{1,0:T(8,128)(2,1)S(1)}, bf16[256,512]{1,0:T(8,128)(2,1)S(1)}, u32[]{:S(2)}, u32[]{:S(2)}) collective-permute-start(bf16[256,512]{1,0:T(8,128)(2,1)S(1)} %get-tuple-element.59.a_0), channel_id=1, source_target_pairs={{0,8},{8,16},{16,24},{24,0},{32,40},{40,48},{48,56},{56,32},{64,72... | collective-permute-start | bytes 786440 | tf_op jit(solution)/shard_map/ppermute | solution.py:41
  35.8 25.7 %collective-permute-start.19 = (bf16[256,512]{1,0:T(8,128)(2,1)S(1)}, bf16[256,512]{1,0:T(8,128)(2,1)S(1)}, u32[]{:S(2)}, u32[]{:S(2)}) collective-permute-start(bf16[256,512]{1,0:T(8,128)(2,1)S(1)} %get-tuple-element.59.a_0), channel_id=1, source_target_pairs={{0,24},{8,0},{16,8},{24,16},{32,56},{40,32},{48,40},{56,48},{64,88... | collective-permute-start | bytes 786440 | tf_op jit(solution)/shard_map/ppermute | solution.py:41
  39.6 22.1 %collective-permute-start.29 = (bf16[256,512]{1,0:T(8,128)(2,1)S(1)}, bf16[256,512]{1,0:T(8,128)(2,1)S(1)}, u32[]{:S(2)}, u32[]{:S(2)}) collective-permute-start(bf16[256,512]{1,0:T(8,128)(2,1)S(1)} %get-tuple-element.60.a_0), channel_id=1, source_target_pairs={{0,8},{8,16},{16,24},{24,0},{32,40},{40,48},{48,56},{56,32},{64,72... | collective-permute-start | bytes 786440 | tf_op jit(solution)/shard_map/ppermute | solution.py:41
  41.9 9.7 %collective-permute-start.2 = (bf16[128,768]{1,0:T(8,128)(2,1)S(1)}, bf16[128,768]{1,0:T(8,128)(2,1)S(1)}, u32[]{:S(2)}, u32[]{:S(2)}) collective-permute-start(bf16[128,768]{1,0:T(8,128)(2,1)S(1)} %slice.52), channel_id=1, source_target_pairs={{0,8},{8,16},{16,24},{24,0},{32,40},{40,48},{48,56},{56,32},{64,72... | collective-permute-start | bytes 589832 | tf_op jit(solution)/shard_map/ppermute | solution.py:41
  51.6 11.9 %collective-permute-start.28 = (bf16[256,512]{1,0:T(8,128)(2,1)S(1)}, bf16[256,512]{1,0:T(8,128)(2,1)S(1)}, u32[]{:S(2)}, u32[]{:S(2)}) collective-permute-start(bf16[256,512]{1,0:T(8,128)(2,1)S(1)} %get-tuple-element.60.a_0), channel_id=1, source_target_pairs={{0,24},{8,0},{16,8},{24,16},{32,56},{40,32},{48,40},{56,48},{64,88... | collective-permute-start | bytes 786440 | tf_op jit(solution)/shard_map/ppermute | solution.py:41
  57.9 21.6 %collective-permute-start.14 = (bf16[272,768]{1,0:T(8,128)(2,1)S(1)}, bf16[272,768]{1,0:T(8,128)(2,1)S(1)}, u32[]{:S(2)}, u32[]{:S(2)}) collective-permute-start(bf16[272,768]{1,0:T(8,128)(2,1)S(1)} %get-tuple-element.33), channel_id=1, source_target_pairs={{0,32},{8,40},{16,48},{24,56},{32,64},{40,72},{48,80},{56,88},{64,... | collective-permute-start | bytes 1253384 | tf_op jit(solution)/shard_map/ppermute | solution.py:45
  61.7 19.7 %collective-permute-start.15 = (bf16[272,768]{1,0:T(8,128)(2,1)S(1)}, bf16[272,768]{1,0:T(8,128)(2,1)S(1)}, u32[]{:S(2)}, u32[]{:S(2)}) collective-permute-start(bf16[272,768]{1,0:T(8,128)(2,1)S(1)} %get-tuple-element.34), channel_id=1, source_target_pairs={{0,96},{8,104},{16,112},{24,120},{32,0},{40,8},{48,16},{56,24},{64... | collective-permute-start | bytes 1253384 | tf_op jit(solution)/shard_map/ppermute | solution.py:45
  63.5 10.3 %collective-permute-start.30 = (bf16[128,512]{1,0:T(8,128)(2,1)S(1)}, bf16[128,512]{1,0:T(8,128)(2,1)S(1)}, u32[]{:S(2)}, u32[]{:S(2)}) collective-permute-start(bf16[128,512]{1,0:T(8,128)(2,1)S(1)} %slice.60), channel_id=1, source_target_pairs={{0,8},{8,16},{16,24},{24,0},{32,40},{40,48},{48,56},{56,32},{64,72... | collective-permute-start | bytes 393224 | tf_op jit(solution)/shard_map/ppermute | solution.py:41
  71.2 11.1 %collective-permute-start.23 = (bf16[272,512]{1,0:T(8,128)(2,1)S(1)}, bf16[272,512]{1,0:T(8,128)(2,1)S(1)}, u32[]{:S(2)}, u32[]{:S(2)}) collective-permute-start(bf16[272,512]{1,0:T(8,128)(2,1)S(1)} %get-tuple-element.42), channel_id=1, source_target_pairs={{0,32},{8,40},{16,48},{24,56},{32,64},{40,72},{48,80},{56,88},{64,... | collective-permute-start | bytes 835592 | tf_op jit(solution)/shard_map/ppermute | solution.py:45
  73.8 11.6 %collective-permute-start.24 = (bf16[272,512]{1,0:T(8,128)(2,1)S(1)}, bf16[272,512]{1,0:T(8,128)(2,1)S(1)}, u32[]{:S(2)}, u32[]{:S(2)}) collective-permute-start(bf16[272,512]{1,0:T(8,128)(2,1)S(1)} %get-tuple-element.43), channel_id=1, source_target_pairs={{0,96},{8,104},{16,112},{24,120},{32,0},{40,8},{48,16},{56,24},{64... | collective-permute-start | bytes 835592 | tf_op jit(solution)/shard_map/ppermute | solution.py:45
  77.8 11.0 %collective-permute-start.32 = (bf16[272,512]{1,0:T(8,128)(2,1)S(1)}, bf16[272,512]{1,0:T(8,128)(2,1)S(1)}, u32[]{:S(2)}, u32[]{:S(2)}) collective-permute-start(bf16[272,512]{1,0:T(8,128)(2,1)S(1)} %get-tuple-element.51), channel_id=1, source_target_pairs={{0,32},{8,40},{16,48},{24,56},{32,64},{40,72},{48,80},{56,88},{64,... | collective-permute-start | bytes 835592 | tf_op jit(solution)/shard_map/ppermute | solution.py:45
  79.5 9.7 %collective-permute-start.33 = (bf16[272,512]{1,0:T(8,128)(2,1)S(1)}, bf16[272,512]{1,0:T(8,128)(2,1)S(1)}, u32[]{:S(2)}, u32[]{:S(2)}) collective-permute-start(bf16[272,512]{1,0:T(8,128)(2,1)S(1)} %get-tuple-element.52), channel_id=1, source_target_pairs={{0,96},{8,104},{16,112},{24,120},{32,0},{40,8},{48,16},{56,24},{64... | collective-permute-start | bytes 835592 | tf_op jit(solution)/shard_map/ppermute | solution.py:45
  82.1 10.9 %collective-permute-start.16 = (bf16[144,768]{1,0:T(8,128)(2,1)S(1)}, bf16[144,768]{1,0:T(8,128)(2,1)S(1)}, u32[]{:S(2)}, u32[]{:S(2)}) collective-permute-start(bf16[144,768]{1,0:T(8,128)(2,1)S(1)} %get-tuple-element.37), channel_id=1, source_target_pairs={{0,32},{8,40},{16,48},{24,56},{32,64},{40,72},{48,80},{56,88},{64,... | collective-permute-start | bytes 663560 | tf_op jit(solution)/shard_map/ppermute | solution.py:45
  82.3 11.6 %collective-permute-start.17 = (bf16[144,768]{1,0:T(8,128)(2,1)S(1)}, bf16[144,768]{1,0:T(8,128)(2,1)S(1)}, u32[]{:S(2)}, u32[]{:S(2)}) collective-permute-start(bf16[144,768]{1,0:T(8,128)(2,1)S(1)} %get-tuple-element.38), channel_id=1, source_target_pairs={{0,96},{8,104},{16,112},{24,120},{32,0},{40,8},{48,16},{56,24},{64... | collective-permute-start | bytes 663560 | tf_op jit(solution)/shard_map/ppermute | solution.py:45
  85.9 10.6 %collective-permute-start.25 = (bf16[144,512]{1,0:T(8,128)(2,1)S(1)}, bf16[144,512]{1,0:T(8,128)(2,1)S(1)}, u32[]{:S(2)}, u32[]{:S(2)}) collective-permute-start(bf16[144,512]{1,0:T(8,128)(2,1)S(1)} %get-tuple-element.46), channel_id=1, source_target_pairs={{0,32},{8,40},{16,48},{24,56},{32,64},{40,72},{48,80},{56,88},{64,... | collective-permute-start | bytes 442376 | tf_op jit(solution)/shard_map/ppermute | solution.py:45
  94.8 10.7 %collective-permute-start.18 = (bf16[144,768]{1,0:T(8,128)(2,1)S(1)}, bf16[144,768]{1,0:T(8,128)(2,1)S(1)}, u32[]{:S(2)}, u32[]{:S(2)}) collective-permute-start(bf16[144,768]{1,0:T(8,128)(2,1)S(1)} %get-tuple-element.40), channel_id=1, source_target_pairs={{0,128},{8,136},{16,144},{24,152},{32,160},{40,168},{48,176},{56,1... | collective-permute-start | bytes 663560 | tf_op jit(solution)/shard_map/ppermute | solution.py:49
  (16 other events, 112.2 us)

commit v2 on v0

v2 whole, which is shorter than its diff:
```python
import functools

import jax
import jax.numpy as jnp
from jax import lax
from jax.experimental import pallas as pl
from jax.experimental.pallas import tpu as pltpu
from jax.sharding import PartitionSpec as P

LEN = 128
NX, NY, NZ = 4, 4, 4
TILE = 256
LANES = 128
CHUNKS = ((512, "abz"), (512, "baz"), (512, "zab"), (256, "abz"))
CODE_TOP = 2.0**14
LEAST = 2.0**-120
VMEM = 16 * 1024 * 1024


def dp_index(z, x, y):
    return (z % 2) * NX * NY + (x % NX) * NY + (y % NY)


def swap(array, z=0, x=0, y=0):
    pairs = [
        (dp_index(k, i, j), dp_index(k ^ z, i ^ x, j ^ y))
        for k in range(2)
        for i in range(NX)
        for j in range(NY)
    ]
    return lax.ppermute(array, "dp", pairs)


FOLDS = {"z": {"z": 1}, "a": {"x": 1}, "b": {"x": 3}}


def tensor_moves(dz, flip):
    return [
        (2 * z + c, 2 * ((z + dz) % NZ) + (c ^ flip))
        for z in range(NZ)
        for c in range(2)
    ]


def from_y(array, offset):
    pairs = [
        (dp_index(k, i, j), dp_index(k, i, j - offset))
        for k in range(2)
        for i in range(NX)
        for j in range(NY)
    ]
    return lax.ppermute(array, "dp", pairs)


def from_z(array, offset):
    return lax.ppermute(array, "tensor", tensor_moves(-offset, 0))


def from_core(array):
    return lax.ppermute(array, "tensor", tensor_moves(0, 1))


def after(later, *earlier):
    return lax.optimization_barrier((later, *earlier))[0]


def put(ref, parts):
    pieces = [p[:, n : n + LANES] for p in parts for n in range(0, TILE, LANES)]
    tops = [jnp.max(p, axis=0, keepdims=True) for p in pieces]
    top = functools.reduce(jnp.maximum, tops)
    top = jnp.maximum(top, LEAST).astype(jnp.bfloat16).astype(jnp.float32)
    inverse = 1.0 / top
    row = 0
    for piece in pieces:
        scaled = piece * inverse * CODE_TOP
        scaled = scaled * scaled
        scaled = scaled * scaled
        scaled = scaled * scaled
        ref[0, row : row + piece.shape[0], :] = scaled.astype(jnp.bfloat16)
        row += piece.shape[0]
    ref[0, row:, :] = jnp.broadcast_to(top, (16, LANES)).astype(jnp.bfloat16)


def get(ref, start, rows):
    scale = ref[0, -16:, :].astype(jnp.float32)[:1] * (1.0 / CODE_TOP)
    found = []
    for n in range(TILE // LANES):
        code = ref[0, start + n * rows : start + (n + 1) * rows, :]
        value = jnp.maximum(code.astype(jnp.float32), 2.0**-126)
        found.append(jnp.exp(jnp.log(value) * 0.125) * scale)
    return jnp.concatenate(found, axis=1)


def message(rows, features):
    return (features // TILE, rows * (TILE // LANES) + 16, LANES)


def squares(slot, grads, acts):
    own, after_y, far_a, far_b, before_y = acts
    total = None
    for e, pair in enumerate(
        (
            (own[:LEN, :], own[LEN:, :]),
            (after_y[:LEN, :], after_y[LEN:, :]),
            (far_a[...], far_b[...]),
            (before_y[:LEN, :], before_y[LEN:, :]),
        )
    ):
        for s in range(2):
            found = jnp.dot(
                grads[slot, e, :, s * LEN : (s + 1) * LEN],
                pair[s],
                preferred_element_type=jnp.float32,
            )
            total = found * found if total is None else total + found * found
    return total


def sums_kernel(run, slots, *refs):
    *acts, grads, kept, sent = refs
    put(sent, [squares(slots[8 * run + n], grads, acts) for n in range(4, 8)])
    for n in range(4):
        block = squares(slots[8 * run + n], grads, acts)
        kept[n * LEN : (n + 1) * LEN, :] = block


def fold_kernel(slots, mine, received, kept, sent):
    half = kept.shape[0] // LEN
    rows = LEN * (TILE // LANES)

    def block(n):
        return mine[n * LEN : (n + 1) * LEN, :] + get(received, n * rows, LEN)

    put(sent, [block(n) for n in range(half, 2 * half)])
    for n in range(half):
        kept[n * LEN : (n + 1) * LEN, :] = block(n)


def final_kernel(mine, received, *refs):
    refs[-1][...] = (mine[...] + get(received, 0, LEN)).T


def spec_of(shape, start):
    if len(shape) == 3:
        return pl.BlockSpec((1,) + shape[1:], lambda i, s: (i, 0, 0))
    return pl.BlockSpec((shape[0], TILE), lambda i, s: (0, i + start))


def call(body, name, features, scalars, ins, outs, cost):
    return pl.pallas_call(
        body,
        name=name,
        grid_spec=pltpu.PrefetchScalarGridSpec(
            num_scalar_prefetch=1,
            grid=(features // TILE,),
            in_specs=[
                pl.BlockSpec(a.shape, lambda i, s: (0, 0, 0, 0))
                if a.ndim == 4
                else spec_of(a.shape, start)
                for a, start in ins
            ],
            out_specs=[spec_of(shape, 0) for shape, _ in outs],
        ),
        out_shape=[jax.ShapeDtypeStruct(shape, dtype) for shape, dtype in outs],
        compiler_params=pltpu.CompilerParams(vmem_limit_bytes=VMEM),
        cost_estimate=pl.CostEstimate(
            flops=cost, bytes_accessed=1, transcendentals=0
        ),
    )(scalars, *[a for a, _ in ins])


def sums(run, slots, acts, grads, start, features):
    outs = (
        ((4 * LEN, features), jnp.float32),
        (message(4 * LEN, features), jnp.bfloat16),
    )
    ins = [(a, start // TILE) for a in acts] + [(grads, 0)]
    cost = 2 * 1024 * 1024 * features
    body = functools.partial(sums_kernel, run)
    return call(body, "sums", features, slots, ins, outs, cost)


def fold(slots, mine, received):
    rows, features = mine.shape[0] // 2, mine.shape[1]
    outs = (
        ((rows, features), jnp.float32),
        (message(rows, features), jnp.bfloat16),
    )
    return call(fold_kernel, "fold", features, slots, [(mine, 0), (received, 0)], outs, 1)


def final(mine, received, start, total, before):
    first = start // TILE
    ins = (mine, received) if before is None else (mine, received, before)
    specs = [
        pl.BlockSpec((LEN, TILE), lambda i: (0, i)),
        pl.BlockSpec((1,) + received.shape[1:], lambda i: (i, 0, 0)),
        pl.BlockSpec(memory_space=pl.ANY),
    ]
    return pl.pallas_call(
        final_kernel,
        name="final",
        grid=(mine.shape[1] // TILE,),
        in_specs=specs[: len(ins)],
        out_specs=pl.BlockSpec((TILE, LEN), lambda i: (i + first, 0)),
        out_shape=jax.ShapeDtypeStruct((total, LEN), jnp.float32),
        input_output_aliases={} if before is None else {2: 0},
        compiler_params=pltpu.CompilerParams(vmem_limit_bytes=VMEM),
    )(*ins)


def per_device(activations, out_grads):
    dp, tensor = lax.axis_index("dp"), lax.axis_index("tensor")
    z_lo, x, y = dp // (NX * NY), (dp // NY) % NX, dp % NY
    z_hi, core = tensor // 2, tensor % 2

    def slots_of(order):
        slots = []
        for n in range(8):
            bits = {d: (n >> (2 - i)) & 1 for i, d in enumerate(order)}
            wanted = (z_lo ^ bits["z"]) * NX + (x ^ bits["a"] ^ (3 * bits["b"]))
            slots.append(((wanted // 2 - z_hi) % NZ) * 2 + (wanted + core) % 2)
        return slots

    slots = [slot for _, order in CHUNKS for slot in slots_of(order)]
    slots = jnp.stack(slots).astype(jnp.int32)
    turned = out_grads.T
    width = turned.shape[0] // NY

    def block_for(offset):
        start = ((y + offset) % NY) * width
        return lax.dynamic_slice_in_dim(turned, start, width, axis=0)

    mine = jnp.stack([block_for(0)] + [from_y(block_for(-o), o) for o in range(1, NY)])
    mine, slots = lax.optimization_barrier((mine, slots))
    after_y, before_y = from_y(activations, 1), from_y(activations, -1)
    z_up, z_down = from_z(mine, 1), from_z(mine, -1)
    other_mine = from_core(mine)
    near = jnp.stack([z_up, z_down])
    far = jnp.concatenate([from_z(near[1, :2], -1), from_z(near[0, 2:], 1)])
    far_a, far_b = from_y(before_y[:LEN], -1), from_y(after_y[LEN:], 1)
    other_near = from_core(near)
    far = after(far, far_a, far_b)
    other_far = from_core(far)
    grads = jnp.stack(
        [mine, other_mine, near[0], other_near[0]]
        + [far, other_far, near[1], other_near[1]]
    )
    acts = (activations, after_y, far_a, far_b, before_y)

    start, runs = 0, []
    for run, (features, order) in enumerate(CHUNKS):
        kept, sent = sums(run, slots, acts, grads, start, features)
        slots = after(slots, kept)
        runs.append((start, order, kept, swap(sent, **FOLDS[order[0]])))
        start += features
    for step in (1, 2):
        for n, (first, order, kept, received) in enumerate(runs):
            kept, sent = fold(slots, kept, received)
            slots = after(slots, kept)
            received = swap(sent, **FOLDS[order[step]])
            runs[n] = (first, order, kept, received)
    result = None
    for first, _, kept, received in runs:
        result = final(kept, received, first, start, result)
    return result


def solution(mesh):
    in_specs = (P("dp", "tensor"), P("dp", "tensor"))
    out_specs = P("tensor", "dp")
    return jax.shard_map(
        per_device, mesh=mesh, in_specs=in_specs, out_specs=out_specs, check_vma=False
    )
```

time: 441 us -> 94.9 us (0.22); the launches traced: 435 us -> 94.8 us
  waiting for transfers between devices: 359 us -> 30 us
  starting transfers between devices: 0.04 us -> 39.1 us
  matrix products: 33.2 us -> 0 us
  local copies, waits for them, and re-layouts: 29.5 us -> 1.73 us
  Pallas kernels: 0 us -> 23.4 us
  between operations: 13.4 us -> 0.4 us
    reduce_scatter x1 -> x0, waiting for transfers between devices: 317 us -> none  [per_device(): owned = lax.psum_scatter(total, 'dp', scatter_dimension=0, tiled=True)]
    all_gather x1 -> x0, waiting for transfers between devices: 41.2 us -> none  [per_device(): gathered = lax.all_gather(out_grads, 'tensor', axis=1, tiled=True)]
    ppermute x0 -> x26, starting transfers between devices: none -> 39.1 us  [the longest x12 16.5 us: swap(): return lax.ppermute(array, 'dp', pairs)]
    dot_general x2 -> x0, matrix products: 33.2 us -> none  [add_sequence(): grads = jnp.dot(pair[0].T, pair[1], preferred_element_type=jnp.float32)]
    ppermute x0 -> x26, waiting for transfers between devices: none -> 30 us  [the longest x7 11.6 us: from_y(): return lax.ppermute(array, 'dp', pairs)]
    while x1 -> x0, local copies, waits for them, and re-layouts: 29.5 us -> none  [per_device(): total, unused = lax.scan(add_sequence, start_total, (grads_seq, inputs_seq))]
    pallas_call x0 -> x16, Pallas kernels: none -> 23.4 us  [the longest x12 19.8 us: call(): pl.pallas_call(body, name=name, grid_spec=pltpu.PrefetchScalarGridSpec(nu...]
  transfers between devices with their start and end apart: 2 -> 26, of which waited for: 2 -> 12; matrix products, arithmetic and copies ran while one was open for 0% -> 1% of each run, Pallas kernels for 0% -> 20%
where the time goes in v2:
time: 94.9 us; the launch traced here: 94.8 us
  starting transfers between devices  39.1 us (41%)
  waiting for transfers between devices  30 us (32%)
  Pallas kernels  23.4 us (25%)
  local copies, waits for them, and re-layouts  1.73 us (2%)
    pallas_call x12, Pallas kernels, call(): pl.pallas_call(body, name=name, grid_spec=pltpu.PrefetchScalarGridSpec(nu...  19.8 us
    ppermute x12, starting transfers between devices, swap(): return lax.ppermute(array, 'dp', pairs)  16.5 us
    ppermute x4, starting transfers between devices, from_z(): return lax.ppermute(array, 'tensor', tensor_moves(-offset, 0))  14.1 us
    ppermute x7, waiting for transfers between devices, from_y(): return lax.ppermute(array, 'dp', pairs)  11.6 us
    ppermute x4, waiting for transfers between devices, from_z(): return lax.ppermute(array, 'tensor', tensor_moves(-offset, 0))  9.64 us
    ppermute x7, starting transfers between devices, from_y(): return lax.ppermute(array, 'dp', pairs)  8.48 us
    ppermute x12, waiting for transfers between devices, swap(): return lax.ppermute(array, 'dp', pairs)  7.25 us
    pallas_call x4, Pallas kernels, final(): pl.pallas_call(final_kernel, name='final', grid=(mine.shape[1] // TILE,),...  3.66 us
  transfers between devices with their start and end apart: 26, of which 12 were waited for; matrix products, arithmetic and copies ran while one was open for 1% of the time, Pallas kernels for 20%

profile of v2, /device:TPU:24, one launch (start us, length us, event | category | flops | bytes accessed | tf_op | source)
XLA Modules:
  0.0 94.8 jit_solution(18055815039317298189)
XLA Ops:
  1.1 2.0 %collective-permute-start.2 = (bf16[128,256]{1,0:T(8,128)(2,1)S(1)}, bf16[128,256]{1,0:T(8,128)(2,1)S(1)}, u32[]{:S(2)}, u32[]{:S(2)}) collective-permute-start(bf16[128,256]{1,0:T(8,128)(2,1)S(1)} %bitcast.38), channel_id=1, source_target_pairs={{0,8},{8,16},{16,24},{24,0},{32,40},{40,48},{48,56},{56,32},{64,72... | collective-permute-start | bytes 196616 | tf_op jit(solution)/shard_map/ppermute | solution.py:52
  5.0 2.0 %collective-permute-start.4 = (bf16[256,1792]{1,0:T(8,128)(2,1)}, bf16[256,1792]{1,0:T(8,128)(2,1)S(1)}, u32[]{:S(2)}, u32[]{:S(2)}) collective-permute-start(bf16[256,1792]{1,0:T(8,128)(2,1)} %refs_0_.7), channel_id=1, source_target_pairs={{0,8},{8,16},{16,24},{24,0},{32,40},{40,48},{48,56},{56,32},{64,72... | collective-permute-start | bytes 2752520 | tf_op jit(solution)/shard_map/ppermute | solution.py:52
  10.1 3.3 %collective-permute-start.9 = (bf16[4,128,256]{2,1,0:T(8,128)(2,1)S(1)}, bf16[4,128,256]{2,1,0:T(8,128)(2,1)S(1)}, u32[]{:S(2)}, u32[]{:S(2)}) collective-permute-start(bf16[4,128,256]{2,1,0:T(8,128)(2,1)S(1)} %pad_maximum_fusion.1), channel_id=1, source_target_pairs={{0,2},{1,3},{2,4},{3,5},{4,6},{5,7},{6,0},{7,1},{8,10},{9,11},{10,... | collective-permute-start | bytes 786440 | tf_op jit(solution)/shard_map/ppermute | solution.py:56
  13.4 3.1 %collective-permute-start.8 = (bf16[4,128,256]{2,1,0:T(8,128)(2,1)S(1)}, bf16[4,128,256]{2,1,0:T(8,128)(2,1)S(1)}, u32[]{:S(2)}, u32[]{:S(2)}) collective-permute-start(bf16[4,128,256]{2,1,0:T(8,128)(2,1)S(1)} %pad_maximum_fusion.1), channel_id=1, source_target_pairs={{0,6},{1,7},{2,0},{3,1},{4,2},{5,3},{6,4},{7,5},{8,14},{9,15},{10,... | collective-permute-start | bytes 786440 | tf_op jit(solution)/shard_map/ppermute | solution.py:56
  16.6 5.9 %collective-permute-done.9 = bf16[4,128,256]{2,1,0:T(8,128)(2,1)S(1)} collective-permute-done((bf16[4,128,256]{2,1,0:T(8,128)(2,1)S(1)}, bf16[4,128,256]{2,1,0:T(8,128)(2,1)S(1)}, u32[]{:S(2)}, u32[]{:S(2)}) %collective-permute-start.9) | collective-permute-done | bytes 262176 | tf_op jit(solution)/shard_map/ppermute | solution.py:56
  22.5 5.3 %collective-permute-start.11 = (bf16[2,128,256]{2,1,0:T(8,128)(2,1)S(1)}, bf16[2,128,256]{2,1,0:T(8,128)(2,1)S(1)}, u32[]{:S(2)}, u32[]{:S(2)}) collective-permute-start(bf16[2,128,256]{2,1,0:T(8,128)(2,1)S(1)} %slice_bitcast_fusion.1), channel_id=1, source_target_pairs={{0,2},{1,3},{2,4},{3,5},{4,6},{5,7},{6,0},{7,1},{8,10},{9,11},{10,... | collective-permute-start | bytes 393224 | tf_op jit(solution)/shard_map/ppermute | solution.py:56
  27.8 2.3 %collective-permute-start.12 = (bf16[2,128,256]{2,1,0:T(8,128)(2,1)S(1)}, bf16[2,128,256]{2,1,0:T(8,128)(2,1)S(1)}, u32[]{:S(2)}, u32[]{:S(2)}) collective-permute-start(bf16[2,128,256]{2,1,0:T(8,128)(2,1)S(1)} %slice_bitcast_fusion), channel_id=1, source_target_pairs={{0,6},{1,7},{2,0},{3,1},{4,2},{5,3},{6,4},{7,5},{8,14},{9,15},{10,... | collective-permute-start | bytes 393224 | tf_op jit(solution)/shard_map/ppermute | solution.py:56
  33.0 3.4 %collective-permute-done.12 = bf16[2,128,256]{2,1,0:T(8,128)(2,1)S(1)} collective-permute-done((bf16[2,128,256]{2,1,0:T(8,128)(2,1)S(1)}, bf16[2,128,256]{2,1,0:T(8,128)(2,1)S(1)}, u32[]{:S(2)}, u32[]{:S(2)}) %collective-permute-start.12) | collective-permute-done | bytes 131104 | tf_op jit(solution)/shard_map/ppermute | solution.py:56
  36.4 6.9 %collective-permute-done.5.refs_2_ = bf16[128,1792]{1,0:T(8,128)(2,1)S(1)} collective-permute-done((bf16[128,1792]{1,0:T(8,128)(2,1)S(1)}, bf16[128,1792]{1,0:T(8,128)(2,1)S(1)}, u32[]{:S(2)}, u32[]{:S(2)}) %collective-permute-start.5) | collective-permute-done | bytes 458784 | tf_op jit(solution)/shard_map/ppermute | solution.py:52
  43.3 2.5 %collective-permute-done.6.refs_3_ = bf16[128,1792]{1,0:T(8,128)(2,1)S(1)} collective-permute-done((bf16[128,1792]{1,0:T(8,128)(2,1)S(1)}, bf16[128,1792]{1,0:T(8,128)(2,1)S(1)}, u32[]{:S(2)}, u32[]{:S(2)}) %collective-permute-start.6) | collective-permute-done | bytes 458784 | tf_op jit(solution)/shard_map/ppermute | solution.py:52
  47.5 3.5 %sums.4 = (f32[512,512]{1,0:T(8,128)S(1)}, bf16[2,1040,128]{2,1,0:T(8,128)(2,1)S(1)}) custom-call(s32[32]{0:T(128)S(1)} %stack.103.slots, bf16[256,1792]{1,0:T(8,128)(2,1)S(1)} %copy-done, bf16[256,1792]{1,0:T(8,128)(2,1)S(1)} %collective-permute-done.3.refs_1_, bf16[128,1792]{1,0:T(8,128)(2,1)S(1)} %collective-permute-done.5.refs_2_, ...), custom_call_target="tpu_custom_call" | custom-call | flops 1073741824 | bytes 1 | tf_op jit(solution)/shard_map/sums/pallas_call | solution.py:150
  50.9 1.6 %collective-permute-start.14 = (bf16[2,1040,128]{2,1,0:T(8,128)(2,1)S(1)}, bf16[2,1040,128]{2,1,0:T(8,128)(2,1)S(1)}, u32[]{:S(2)}, u32[]{:S(2)}) collective-permute-start(bf16[2,1040,128]{2,1,0:T(8,128)(2,1)S(1)} %get-tuple-element.54), channel_id=1, source_target_pairs={{0,32},{8,40},{16,48},{24,56},{32,0},{40,8},{48,16},{56,24},{64,96... | collective-permute-start | bytes 1597448 | tf_op jit(solution)/shard_map/ppermute | solution.py:31
  52.5 3.5 %sums.5 = (f32[512,512]{1,0:T(8,128)S(1)}, bf16[2,1040,128]{2,1,0:T(8,128)(2,1)S(1)}) custom-call(s32[32]{0:T(128)S(1)} %stack.103.slots, bf16[256,1792]{1,0:T(8,128)(2,1)S(1)} %copy-done, bf16[256,1792]{1,0:T(8,128)(2,1)S(1)} %collective-permute-done.3.refs_1_, bf16[128,1792]{1,0:T(8,128)(2,1)S(1)} %collective-permute-done.5.refs_2_, ...), custom_call_target="tpu_custom_call" | custom-call | flops 1073741824 | bytes 1 | tf_op jit(solution)/shard_map/sums/pallas_call | solution.py:150
  56.0 2.2 %collective-permute-start.15 = (bf16[2,1040,128]{2,1,0:T(8,128)(2,1)S(1)}, bf16[2,1040,128]{2,1,0:T(8,128)(2,1)S(1)}, u32[]{:S(2)}, u32[]{:S(2)}) collective-permute-start(bf16[2,1040,128]{2,1,0:T(8,128)(2,1)S(1)} %get-tuple-element.57), channel_id=1, source_target_pairs={{0,96},{8,104},{16,112},{24,120},{32,64},{40,72},{48,80},{56,88},{... | collective-permute-start | bytes 1597448 | tf_op jit(solution)/shard_map/ppermute | solution.py:31
  58.2 3.5 %sums.6 = (f32[512,512]{1,0:T(8,128)S(1)}, bf16[2,1040,128]{2,1,0:T(8,128)(2,1)S(1)}) custom-call(s32[32]{0:T(128)S(1)} %stack.103.slots, bf16[256,1792]{1,0:T(8,128)(2,1)S(1)} %copy-done, bf16[256,1792]{1,0:T(8,128)(2,1)S(1)} %collective-permute-done.3.refs_1_, bf16[128,1792]{1,0:T(8,128)(2,1)S(1)} %collective-permute-done.5.refs_2_, ...), custom_call_target="tpu_custom_call" | custom-call | flops 1073741824 | bytes 1 | tf_op jit(solution)/shard_map/sums/pallas_call | solution.py:150
  61.6 1.7 %collective-permute-start.16 = (bf16[2,1040,128]{2,1,0:T(8,128)(2,1)S(1)}, bf16[2,1040,128]{2,1,0:T(8,128)(2,1)S(1)}, u32[]{:S(2)}, u32[]{:S(2)}) collective-permute-start(bf16[2,1040,128]{2,1,0:T(8,128)(2,1)S(1)} %get-tuple-element.60), channel_id=1, source_target_pairs={{0,128},{8,136},{16,144},{24,152},{32,160},{40,168},{48,176},{56,1... | collective-permute-start | bytes 1597448 | tf_op jit(solution)/shard_map/ppermute | solution.py:31
  63.3 1.9 %sums.7 = (f32[512,256]{1,0:T(8,128)S(1)}, bf16[1,1040,128]{2,1,0:T(8,128)(2,1)S(1)}) custom-call(s32[32]{0:T(128)S(1)} %stack.103.slots, bf16[256,1792]{1,0:T(8,128)(2,1)S(1)} %copy-done, bf16[256,1792]{1,0:T(8,128)(2,1)S(1)} %collective-permute-done.3.refs_1_, bf16[128,1792]{1,0:T(8,128)(2,1)S(1)} %collective-permute-done.5.refs_2_, ...), custom_call_target="tpu_custom_call" | custom-call | flops 536870912 | bytes 1 | tf_op jit(solution)/shard_map/sums/pallas_call | solution.py:150
  67.0 2.1 %collective-permute-start.18 = (bf16[2,528,128]{2,1,0:T(8,128)(2,1)S(1)}, bf16[2,528,128]{2,1,0:T(8,128)(2,1)S(1)}, u32[]{:S(2)}, u32[]{:S(2)}) collective-permute-start(bf16[2,528,128]{2,1,0:T(8,128)(2,1)S(1)} %get-tuple-element.66), channel_id=1, source_target_pairs={{0,96},{8,104},{16,112},{24,120},{32,64},{40,72},{48,80},{56,88},{... | collective-permute-start | bytes 811016 | tf_op jit(solution)/shard_map/ppermute | solution.py:31
  69.2 3.1 %collective-permute-done.15.received = bf16[2,1040,128]{2,1,0:T(8,128)(2,1)S(1)} collective-permute-done((bf16[2,1040,128]{2,1,0:T(8,128)(2,1)S(1)}, bf16[2,1040,128]{2,1,0:T(8,128)(2,1)S(1)}, u32[]{:S(2)}, u32[]{:S(2)}) %collective-permute-start.15) | collective-permute-done | bytes 532512 | tf_op jit(solution)/shard_map/ppermute | solution.py:31
  73.5 1.8 %collective-permute-done.16.received = bf16[2,1040,128]{2,1,0:T(8,128)(2,1)S(1)} collective-permute-done((bf16[2,1040,128]{2,1,0:T(8,128)(2,1)S(1)}, bf16[2,1040,128]{2,1,0:T(8,128)(2,1)S(1)}, u32[]{:S(2)}, u32[]{:S(2)}) %collective-permute-start.16) | collective-permute-done | bytes 532512 | tf_op jit(solution)/shard_map/ppermute | solution.py:31
  80.4 1.8 %collective-permute-done.19.received = bf16[2,528,128]{2,1,0:T(8,128)(2,1)S(1)} collective-permute-done((bf16[2,528,128]{2,1,0:T(8,128)(2,1)S(1)}, bf16[2,528,128]{2,1,0:T(8,128)(2,1)S(1)}, u32[]{:S(2)}, u32[]{:S(2)}) %collective-permute-start.19) | collective-permute-done | bytes 270368 | tf_op jit(solution)/shard_map/ppermute | solution.py:31
  83.1 1.6 %collective-permute-start.24 = (bf16[2,272,128]{2,1,0:T(8,128)(2,1)S(1)}, bf16[2,272,128]{2,1,0:T(8,128)(2,1)S(1)}, u32[]{:S(2)}, u32[]{:S(2)}) collective-permute-start(bf16[2,272,128]{2,1,0:T(8,128)(2,1)S(1)} %get-tuple-element.79), channel_id=1, source_target_pairs={{0,128},{8,136},{16,144},{24,152},{32,160},{40,168},{48,176},{56,1... | collective-permute-start | bytes 417800 | tf_op jit(solution)/shard_map/ppermute | solution.py:31
  86.6 2.0 %collective-permute-start.23 = (bf16[2,272,128]{2,1,0:T(8,128)(2,1)S(1)}, bf16[2,272,128]{2,1,0:T(8,128)(2,1)S(1)}, u32[]{:S(2)}, u32[]{:S(2)}) collective-permute-start(bf16[2,272,128]{2,1,0:T(8,128)(2,1)S(1)} %get-tuple-element.78), channel_id=1, source_target_pairs={{0,96},{8,104},{16,112},{24,120},{32,64},{40,72},{48,80},{56,88},{... | collective-permute-start | bytes 417800 | tf_op jit(solution)/shard_map/ppermute | solution.py:31
  89.4 1.7 %collective-permute-start.22 = (bf16[1,272,128]{2,1,0:T(8,128)(2,1)S(1)}, bf16[1,272,128]{2,1,0:T(8,128)(2,1)S(1)}, u32[]{:S(2)}, u32[]{:S(2)}) collective-permute-start(bf16[1,272,128]{2,1,0:T(8,128)(2,1)S(1)} %get-tuple-element.77), channel_id=1, source_target_pairs={{0,128},{8,136},{16,144},{24,152},{32,160},{40,168},{48,176},{56,1... | collective-permute-start | bytes 208904 | tf_op jit(solution)/shard_map/ppermute | solution.py:31
  (67 shorter events, 25.6 us)
Async XLA Ops:
  1.1 6.9 %collective-permute-start.2 = (bf16[128,256]{1,0:T(8,128)(2,1)S(1)}, bf16[128,256]{1,0:T(8,128)(2,1)S(1)}, u32[]{:S(2)}, u32[]{:S(2)}) collective-permute-start(bf16[128,256]{1,0:T(8,128)(2,1)S(1)} %bitcast.38), channel_id=1, source_target_pairs={{0,8},{8,16},{16,24},{24,0},{32,40},{40,48},{48,56},{56,32},{64,72... | collective-permute-start | bytes 196616 | tf_op jit(solution)/shard_map/ppermute | solution.py:52
  3.2 5.7 %collective-permute-start = (bf16[128,256]{1,0:T(8,128)(2,1)S(1)}, bf16[128,256]{1,0:T(8,128)(2,1)S(1)}, u32[]{:S(2)}, u32[]{:S(2)}) collective-permute-start(bf16[128,256]{1,0:T(8,128)(2,1)S(1)} %bitcast.39), channel_id=1, source_target_pairs={{0,24},{8,0},{16,8},{24,16},{32,56},{40,32},{48,40},{56,48},{64,88... | collective-permute-start | bytes 196616 | tf_op jit(solution)/shard_map/ppermute | solution.py:52
  3.5 6.6 %collective-permute-start.1 = (bf16[128,256]{1,0:T(8,128)(2,1)S(1)}, bf16[128,256]{1,0:T(8,128)(2,1)S(1)}, u32[]{:S(2)}, u32[]{:S(2)}) collective-permute-start(bf16[128,256]{1,0:T(8,128)(2,1)S(1)} %bitcast.40), channel_id=1, source_target_pairs={{0,16},{8,24},{16,0},{24,8},{32,48},{40,56},{48,32},{56,40},{64,80... | collective-permute-start | bytes 196616 | tf_op jit(solution)/shard_map/ppermute | solution.py:52
  5.0 25.2 %collective-permute-start.4 = (bf16[256,1792]{1,0:T(8,128)(2,1)}, bf16[256,1792]{1,0:T(8,128)(2,1)S(1)}, u32[]{:S(2)}, u32[]{:S(2)}) collective-permute-start(bf16[256,1792]{1,0:T(8,128)(2,1)} %refs_0_.7), channel_id=1, source_target_pairs={{0,8},{8,16},{16,24},{24,0},{32,40},{40,48},{48,56},{56,32},{64,72... | collective-permute-start | bytes 2752520 | tf_op jit(solution)/shard_map/ppermute | solution.py:52
  7.0 23.3 %collective-permute-start.3 = (bf16[256,1792]{1,0:T(8,128)(2,1)}, bf16[256,1792]{1,0:T(8,128)(2,1)S(1)}, u32[]{:S(2)}, u32[]{:S(2)}) collective-permute-start(bf16[256,1792]{1,0:T(8,128)(2,1)} %refs_0_.7), channel_id=1, source_target_pairs={{0,24},{8,0},{16,8},{24,16},{32,56},{40,32},{48,40},{56,48},{64,88... | collective-permute-start | bytes 2752520 | tf_op jit(solution)/shard_map/ppermute | solution.py:52
  10.1 12.4 %collective-permute-start.9 = (bf16[4,128,256]{2,1,0:T(8,128)(2,1)S(1)}, bf16[4,128,256]{2,1,0:T(8,128)(2,1)S(1)}, u32[]{:S(2)}, u32[]{:S(2)}) collective-permute-start(bf16[4,128,256]{2,1,0:T(8,128)(2,1)S(1)} %pad_maximum_fusion.1), channel_id=1, source_target_pairs={{0,2},{1,3},{2,4},{3,5},{4,6},{5,7},{6,0},{7,1},{8,10},{9,11},{10,... | collective-permute-start | bytes 786440 | tf_op jit(solution)/shard_map/ppermute | solution.py:56
  13.4 14.3 %collective-permute-start.8 = (bf16[4,128,256]{2,1,0:T(8,128)(2,1)S(1)}, bf16[4,128,256]{2,1,0:T(8,128)(2,1)S(1)}, u32[]{:S(2)}, u32[]{:S(2)}) collective-permute-start(bf16[4,128,256]{2,1,0:T(8,128)(2,1)S(1)} %pad_maximum_fusion.1), channel_id=1, source_target_pairs={{0,6},{1,7},{2,0},{3,1},{4,2},{5,3},{6,4},{7,5},{8,14},{9,15},{10,... | collective-permute-start | bytes 786440 | tf_op jit(solution)/shard_map/ppermute | solution.py:56
  16.5 15.4 %collective-permute-start.7 = (bf16[4,128,256]{2,1,0:T(8,128)(2,1)S(1)}, bf16[4,128,256]{2,1,0:T(8,128)(2,1)S(1)}, u32[]{:S(2)}, u32[]{:S(2)}) collective-permute-start(bf16[4,128,256]{2,1,0:T(8,128)(2,1)S(1)} %pad_maximum_fusion.1), channel_id=1, source_target_pairs={{0,1},{1,0},{2,3},{3,2},{4,5},{5,4},{6,7},{7,6},{8,9},{9,8},{10,11... | collective-permute-start | bytes 786440 | tf_op jit(solution)/shard_map/ppermute | solution.py:60
  22.5 10.5 %collective-permute-start.11 = (bf16[2,128,256]{2,1,0:T(8,128)(2,1)S(1)}, bf16[2,128,256]{2,1,0:T(8,128)(2,1)S(1)}, u32[]{:S(2)}, u32[]{:S(2)}) collective-permute-start(bf16[2,128,256]{2,1,0:T(8,128)(2,1)S(1)} %slice_bitcast_fusion.1), channel_id=1, source_target_pairs={{0,2},{1,3},{2,4},{3,5},{4,6},{5,7},{6,0},{7,1},{8,10},{9,11},{10,... | collective-permute-start | bytes 393224 | tf_op jit(solution)/shard_map/ppermute | solution.py:56
  27.8 8.6 %collective-permute-start.12 = (bf16[2,128,256]{2,1,0:T(8,128)(2,1)S(1)}, bf16[2,128,256]{2,1,0:T(8,128)(2,1)S(1)}, u32[]{:S(2)}, u32[]{:S(2)}) collective-permute-start(bf16[2,128,256]{2,1,0:T(8,128)(2,1)S(1)} %slice_bitcast_fusion), channel_id=1, source_target_pairs={{0,6},{1,7},{2,0},{3,1},{4,2},{5,3},{6,4},{7,5},{8,14},{9,15},{10,... | collective-permute-start | bytes 393224 | tf_op jit(solution)/shard_map/ppermute | solution.py:56
  30.2 15.7 %collective-permute-start.10 = (bf16[2,4,128,256]{3,2,1,0:T(8,128)(2,1)S(1)}, bf16[2,4,128,256]{3,2,1,0:T(8,128)(2,1)S(1)}, u32[]{:S(2)}, u32[]{:S(2)}) collective-permute-start(bf16[2,4,128,256]{3,2,1,0:T(8,128)(2,1)S(1)} %pad_maximum_fusion), channel_id=1, source_target_pairs={{0,1},{1,0},{2,3},{3,2},{4,5},{5,4},{6,7},{7,6},{8,9},{9,8},{10,11... | collective-permute-start | bytes 1572872 | tf_op jit(solution)/shard_map/ppermute | solution.py:60
  30.3 13.0 %collective-permute-start.5 = (bf16[128,1792]{1,0:T(8,128)(2,1)S(1)}, bf16[128,1792]{1,0:T(8,128)(2,1)S(1)}, u32[]{:S(2)}, u32[]{:S(2)}) collective-permute-start(bf16[128,1792]{1,0:T(8,128)(2,1)S(1)} %slice.24), channel_id=1, source_target_pairs={{0,8},{8,16},{16,24},{24,0},{32,40},{40,48},{48,56},{56,32},{64,72... | collective-permute-start | bytes 1376264 | tf_op jit(solution)/shard_map/ppermute | solution.py:52
  31.9 13.9 %collective-permute-start.6 = (bf16[128,1792]{1,0:T(8,128)(2,1)S(1)}, bf16[128,1792]{1,0:T(8,128)(2,1)S(1)}, u32[]{:S(2)}, u32[]{:S(2)}) collective-permute-start(bf16[128,1792]{1,0:T(8,128)(2,1)S(1)} %slice.25), channel_id=1, source_target_pairs={{0,24},{8,0},{16,8},{24,16},{32,56},{40,32},{48,40},{56,48},{64,88... | collective-permute-start | bytes 1376264 | tf_op jit(solution)/shard_map/ppermute | solution.py:52
  50.9 14.9 %collective-permute-start.14 = (bf16[2,1040,128]{2,1,0:T(8,128)(2,1)S(1)}, bf16[2,1040,128]{2,1,0:T(8,128)(2,1)S(1)}, u32[]{:S(2)}, u32[]{:S(2)}) collective-permute-start(bf16[2,1040,128]{2,1,0:T(8,128)(2,1)S(1)} %get-tuple-element.54), channel_id=1, source_target_pairs={{0,32},{8,40},{16,48},{24,56},{32,0},{40,8},{48,16},{56,24},{64,96... | collective-permute-start | bytes 1597448 | tf_op jit(solution)/shard_map/ppermute | solution.py:31
  56.0 16.3 %collective-permute-start.15 = (bf16[2,1040,128]{2,1,0:T(8,128)(2,1)S(1)}, bf16[2,1040,128]{2,1,0:T(8,128)(2,1)S(1)}, u32[]{:S(2)}, u32[]{:S(2)}) collective-permute-start(bf16[2,1040,128]{2,1,0:T(8,128)(2,1)S(1)} %get-tuple-element.57), channel_id=1, source_target_pairs={{0,96},{8,104},{16,112},{24,120},{32,64},{40,72},{48,80},{56,88},{... | collective-permute-start | bytes 1597448 | tf_op jit(solution)/shard_map/ppermute | solution.py:31
  61.6 13.7 %collective-permute-start.16 = (bf16[2,1040,128]{2,1,0:T(8,128)(2,1)S(1)}, bf16[2,1040,128]{2,1,0:T(8,128)(2,1)S(1)}, u32[]{:S(2)}, u32[]{:S(2)}) collective-permute-start(bf16[2,1040,128]{2,1,0:T(8,128)(2,1)S(1)} %get-tuple-element.60), channel_id=1, source_target_pairs={{0,128},{8,136},{16,144},{24,152},{32,160},{40,168},{48,176},{56,1... | collective-permute-start | bytes 1597448 | tf_op jit(solution)/shard_map/ppermute | solution.py:31
  65.2 11.9 %collective-permute-start.17 = (bf16[1,1040,128]{2,1,0:T(8,128)(2,1)S(1)}, bf16[1,1040,128]{2,1,0:T(8,128)(2,1)S(1)}, u32[]{:S(2)}, u32[]{:S(2)}) collective-permute-start(bf16[1,1040,128]{2,1,0:T(8,128)(2,1)S(1)} %get-tuple-element.63), channel_id=1, source_target_pairs={{0,32},{8,40},{16,48},{24,56},{32,0},{40,8},{48,16},{56,24},{64,96... | collective-permute-start | bytes 798728 | tf_op jit(solution)/shard_map/ppermute | solution.py:31
  67.0 12.5 %collective-permute-start.18 = (bf16[2,528,128]{2,1,0:T(8,128)(2,1)S(1)}, bf16[2,528,128]{2,1,0:T(8,128)(2,1)S(1)}, u32[]{:S(2)}, u32[]{:S(2)}) collective-permute-start(bf16[2,528,128]{2,1,0:T(8,128)(2,1)S(1)} %get-tuple-element.66), channel_id=1, source_target_pairs={{0,96},{8,104},{16,112},{24,120},{32,64},{40,72},{48,80},{56,88},{... | collective-permute-start | bytes 811016 | tf_op jit(solution)/shard_map/ppermute | solution.py:31
  73.4 8.8 %collective-permute-start.19 = (bf16[2,528,128]{2,1,0:T(8,128)(2,1)S(1)}, bf16[2,528,128]{2,1,0:T(8,128)(2,1)S(1)}, u32[]{:S(2)}, u32[]{:S(2)}) collective-permute-start(bf16[2,528,128]{2,1,0:T(8,128)(2,1)S(1)} %get-tuple-element.69), channel_id=1, source_target_pairs={{0,32},{8,40},{16,48},{24,56},{32,0},{40,8},{48,16},{56,24},{64,96... | collective-permute-start | bytes 811016 | tf_op jit(solution)/shard_map/ppermute | solution.py:31
  76.4 9.3 %collective-permute-start.20 = (bf16[2,528,128]{2,1,0:T(8,128)(2,1)S(1)}, bf16[2,528,128]{2,1,0:T(8,128)(2,1)S(1)}, u32[]{:S(2)}, u32[]{:S(2)}) collective-permute-start(bf16[2,528,128]{2,1,0:T(8,128)(2,1)S(1)} %get-tuple-element.72), channel_id=1, source_target_pairs={{0,32},{8,40},{16,48},{24,56},{32,0},{40,8},{48,16},{56,24},{64,96... | collective-permute-start | bytes 811016 | tf_op jit(solution)/shard_map/ppermute | solution.py:31
  77.9 10.8 %collective-permute-start.21 = (bf16[1,528,128]{2,1,0:T(8,128)(2,1)S(1)}, bf16[1,528,128]{2,1,0:T(8,128)(2,1)S(1)}, u32[]{:S(2)}, u32[]{:S(2)}) collective-permute-start(bf16[1,528,128]{2,1,0:T(8,128)(2,1)S(1)} %get-tuple-element.75), channel_id=1, source_target_pairs={{0,96},{8,104},{16,112},{24,120},{32,64},{40,72},{48,80},{56,88},{... | collective-permute-start | bytes 405512 | tf_op jit(solution)/shard_map/ppermute | solution.py:31
  83.1 9.0 %collective-permute-start.24 = (bf16[2,272,128]{2,1,0:T(8,128)(2,1)S(1)}, bf16[2,272,128]{2,1,0:T(8,128)(2,1)S(1)}, u32[]{:S(2)}, u32[]{:S(2)}) collective-permute-start(bf16[2,272,128]{2,1,0:T(8,128)(2,1)S(1)} %get-tuple-element.79), channel_id=1, source_target_pairs={{0,128},{8,136},{16,144},{24,152},{32,160},{40,168},{48,176},{56,1... | collective-permute-start | bytes 417800 | tf_op jit(solution)/shard_map/ppermute | solution.py:31
  84.7 6.4 %collective-permute-start.25 = (bf16[2,272,128]{2,1,0:T(8,128)(2,1)S(1)}, bf16[2,272,128]{2,1,0:T(8,128)(2,1)S(1)}, u32[]{:S(2)}, u32[]{:S(2)}) collective-permute-start(bf16[2,272,128]{2,1,0:T(8,128)(2,1)S(1)} %get-tuple-element.80), channel_id=1, source_target_pairs={{0,128},{8,136},{16,144},{24,152},{32,160},{40,168},{48,176},{56,1... | collective-permute-start | bytes 417800 | tf_op jit(solution)/shard_map/ppermute | solution.py:31
  86.6 6.4 %collective-permute-start.23 = (bf16[2,272,128]{2,1,0:T(8,128)(2,1)S(1)}, bf16[2,272,128]{2,1,0:T(8,128)(2,1)S(1)}, u32[]{:S(2)}, u32[]{:S(2)}) collective-permute-start(bf16[2,272,128]{2,1,0:T(8,128)(2,1)S(1)} %get-tuple-element.78), channel_id=1, source_target_pairs={{0,96},{8,104},{16,112},{24,120},{32,64},{40,72},{48,80},{56,88},{... | collective-permute-start | bytes 417800 | tf_op jit(solution)/shard_map/ppermute | solution.py:31
  (3 other events, 21.7 us)

commit v3 on v2

--- a/solution.py
+++ b/solution.py
@@ -116,9 +116,13 @@
     return total
 
 
-def sums_kernel(run, slots, *refs):
-    *acts, grads, kept, sent = refs
+def sent_kernel(run, slots, *refs):
+    *acts, grads, sent = refs
     put(sent, [squares(slots[8 * run + n], grads, acts) for n in range(4, 8)])
+
+
+def kept_kernel(run, slots, *refs):
+    *acts, grads, kept = refs
     for n in range(4):
         block = squares(slots[8 * run + n], grads, acts)
         kept[n * LEN : (n + 1) * LEN, :] = block
@@ -169,15 +173,22 @@
     )(scalars, *[a for a, _ in ins])
 
 
-def sums(run, slots, acts, grads, start, features):
-    outs = (
-        ((4 * LEN, features), jnp.float32),
-        (message(4 * LEN, features), jnp.bfloat16),
-    )
+def sums(body, name, run, slots, acts, grads, start, out):
+    features = CHUNKS[run][0]
     ins = [(a, start // TILE) for a in acts] + [(grads, 0)]
-    cost = 2 * 1024 * 1024 * features
-    body = functools.partial(sums_kernel, run)
-    return call(body, "sums", features, slots, ins, outs, cost)
+    cost = 1024 * 1024 * features
+    body = functools.partial(body, run)
+    return call(body, name, features, slots, ins, (out,), cost)[0]
+
+
+def sent_sums(run, slots, acts, grads, start):
+    out = (message(4 * LEN, CHUNKS[run][0]), jnp.bfloat16)
+    return sums(sent_kernel, "sent_sums", run, slots, acts, grads, start, out)
+
+
+def kept_sums(run, slots, acts, grads, start):
+    out = ((4 * LEN, CHUNKS[run][0]), jnp.float32)
+    return sums(kept_kernel, "kept_sums", run, slots, acts, grads, start, out)
 
 
 def fold(slots, mine, received):
@@ -248,18 +259,27 @@
     )
     acts = (activations, after_y, far_a, far_b, before_y)
 
-    start, runs = 0, []
-    for run, (features, order) in enumerate(CHUNKS):
-        kept, sent = sums(run, slots, acts, grads, start, features)
-        slots = after(slots, kept)
-        runs.append((start, order, kept, swap(sent, **FOLDS[order[0]])))
-        start += features
+    starts = [sum(f for f, _ in CHUNKS[:n]) for n in range(len(CHUNKS))]
+    start = sum(f for f, _ in CHUNKS)
+    received, kept = {}, {}
+    for run, (_, order) in enumerate(CHUNKS):
+        sent = sent_sums(run, slots, acts, grads, starts[run])
+        received[run] = swap(sent, **FOLDS[order[0]])
+        slots = after(slots, sent)
+
+    def keep(run, slots):
+        kept[run] = kept_sums(run, slots, acts, grads, starts[run])
+        return after(slots, kept[run])
+
+    slots = keep(1, keep(0, slots))
     for step in (1, 2):
-        for n, (first, order, kept, received) in enumerate(runs):
-            kept, sent = fold(slots, kept, received)
-            slots = after(slots, kept)
-            received = swap(sent, **FOLDS[order[step]])
-            runs[n] = (first, order, kept, received)
+        for run, (_, order) in enumerate(CHUNKS):
+            kept[run], sent = fold(slots, kept[run], received[run])
+            received[run] = swap(sent, **FOLDS[order[step]])
+            slots = after(slots, kept[run])
+            if run + 2 < len(CHUNKS) and step == 1:
+                slots = keep(run + 2, slots)
+    runs = [(starts[n], None, kept[n], received[n]) for n in range(len(CHUNKS))]
     result = None
     for first, _, kept, received in runs:
         result = final(kept, received, first, start, result)

time: 94.9 us -> 94.3 us (level)
  waiting for transfers between devices: 30 us -> 24.8 us
  Pallas kernels: 23.4 us -> 27.3 us
    ppermute x12, waiting for transfers between devices: 7.25 us -> 2.09 us  [swap(): return lax.ppermute(array, 'dp', pairs)]
    pallas_call x12 -> x16, Pallas kernels: 19.8 us -> 23.6 us  [call(): pl.pallas_call(body, name=name, grid_spec=pltpu.PrefetchScalarGridSpec(nu...]
  transfers between devices with their start and end apart: 26 -> 26, of which waited for: 12 -> 12; matrix products, arithmetic and copies ran while one was open for 1% -> 1% of each run, Pallas kernels for 20% -> 26%
where the time goes in v3:
time: 94.3 us; the launch traced here: 94.1 us
  starting transfers between devices  39.8 us (42%)
  Pallas kernels  27.3 us (29%)
  waiting for transfers between devices  24.8 us (26%)
  local copies, waits for them, and re-layouts  1.73 us (2%)
    pallas_call x16, Pallas kernels, call(): pl.pallas_call(body, name=name, grid_spec=pltpu.PrefetchScalarGridSpec(nu...  23.6 us
    ppermute x12, starting transfers between devices, swap(): return lax.ppermute(array, 'dp', pairs)  17.2 us
    ppermute x4, starting transfers between devices, from_z(): return lax.ppermute(array, 'tensor', tensor_moves(-offset, 0))  14.1 us
    ppermute x7, waiting for transfers between devices, from_y(): return lax.ppermute(array, 'dp', pairs)  11.6 us
    ppermute x4, waiting for transfers between devices, from_z(): return lax.ppermute(array, 'tensor', tensor_moves(-offset, 0))  9.64 us
    ppermute x7, starting transfers between devices, from_y(): return lax.ppermute(array, 'dp', pairs)  8.48 us
    pallas_call x4, Pallas kernels, final(): pl.pallas_call(final_kernel, name='final', grid=(mine.shape[1] // TILE,),...  3.65 us
    ppermute x12, waiting for transfers between devices, swap(): return lax.ppermute(array, 'dp', pairs)  2.09 us
  transfers between devices with their start and end apart: 26, of which 12 were waited for; matrix products, arithmetic and copies ran while one was open for 1% of the time, Pallas kernels for 26%

profile of v3, /device:TPU:24, one launch (start us, length us, event | category | flops | bytes accessed | tf_op | source)
XLA Modules:
  0.0 94.1 jit_solution(17796751423880926860)
XLA Ops:
  1.1 2.0 %collective-permute-start.2 = (bf16[128,256]{1,0:T(8,128)(2,1)S(1)}, bf16[128,256]{1,0:T(8,128)(2,1)S(1)}, u32[]{:S(2)}, u32[]{:S(2)}) collective-permute-start(bf16[128,256]{1,0:T(8,128)(2,1)S(1)} %bitcast.38), channel_id=1, source_target_pairs={{0,8},{8,16},{16,24},{24,0},{32,40},{40,48},{48,56},{56,32},{64,72... | collective-permute-start | bytes 196616 | tf_op jit(solution)/shard_map/ppermute | solution.py:52
  3.5 1.5 %collective-permute-start.1 = (bf16[128,256]{1,0:T(8,128)(2,1)S(1)}, bf16[128,256]{1,0:T(8,128)(2,1)S(1)}, u32[]{:S(2)}, u32[]{:S(2)}) collective-permute-start(bf16[128,256]{1,0:T(8,128)(2,1)S(1)} %bitcast.40), channel_id=1, source_target_pairs={{0,16},{8,24},{16,0},{24,8},{32,48},{40,56},{48,32},{56,40},{64,80... | collective-permute-start | bytes 196616 | tf_op jit(solution)/shard_map/ppermute | solution.py:52
  5.0 2.0 %collective-permute-start.4 = (bf16[256,1792]{1,0:T(8,128)(2,1)}, bf16[256,1792]{1,0:T(8,128)(2,1)S(1)}, u32[]{:S(2)}, u32[]{:S(2)}) collective-permute-start(bf16[256,1792]{1,0:T(8,128)(2,1)} %refs_0_.15), channel_id=1, source_target_pairs={{0,8},{8,16},{16,24},{24,0},{32,40},{40,48},{48,56},{56,32},{64,72... | collective-permute-start | bytes 2752520 | tf_op jit(solution)/shard_map/ppermute | solution.py:52
  10.1 3.3 %collective-permute-start.9 = (bf16[4,128,256]{2,1,0:T(8,128)(2,1)S(1)}, bf16[4,128,256]{2,1,0:T(8,128)(2,1)S(1)}, u32[]{:S(2)}, u32[]{:S(2)}) collective-permute-start(bf16[4,128,256]{2,1,0:T(8,128)(2,1)S(1)} %pad_maximum_fusion.1), channel_id=1, source_target_pairs={{0,2},{1,3},{2,4},{3,5},{4,6},{5,7},{6,0},{7,1},{8,10},{9,11},{10,... | collective-permute-start | bytes 786440 | tf_op jit(solution)/shard_map/ppermute | solution.py:56
  13.4 3.1 %collective-permute-start.8 = (bf16[4,128,256]{2,1,0:T(8,128)(2,1)S(1)}, bf16[4,128,256]{2,1,0:T(8,128)(2,1)S(1)}, u32[]{:S(2)}, u32[]{:S(2)}) collective-permute-start(bf16[4,128,256]{2,1,0:T(8,128)(2,1)S(1)} %pad_maximum_fusion.1), channel_id=1, source_target_pairs={{0,6},{1,7},{2,0},{3,1},{4,2},{5,3},{6,4},{7,5},{8,14},{9,15},{10,... | collective-permute-start | bytes 786440 | tf_op jit(solution)/shard_map/ppermute | solution.py:56
  16.6 5.9 %collective-permute-done.9 = bf16[4,128,256]{2,1,0:T(8,128)(2,1)S(1)} collective-permute-done((bf16[4,128,256]{2,1,0:T(8,128)(2,1)S(1)}, bf16[4,128,256]{2,1,0:T(8,128)(2,1)S(1)}, u32[]{:S(2)}, u32[]{:S(2)}) %collective-permute-start.9) | collective-permute-done | bytes 262176 | tf_op jit(solution)/shard_map/ppermute | solution.py:56
  22.5 5.3 %collective-permute-start.11 = (bf16[2,128,256]{2,1,0:T(8,128)(2,1)S(1)}, bf16[2,128,256]{2,1,0:T(8,128)(2,1)S(1)}, u32[]{:S(2)}, u32[]{:S(2)}) collective-permute-start(bf16[2,128,256]{2,1,0:T(8,128)(2,1)S(1)} %slice_bitcast_fusion.1), channel_id=1, source_target_pairs={{0,2},{1,3},{2,4},{3,5},{4,6},{5,7},{6,0},{7,1},{8,10},{9,11},{10,... | collective-permute-start | bytes 393224 | tf_op jit(solution)/shard_map/ppermute | solution.py:56
  27.8 2.3 %collective-permute-start.12 = (bf16[2,128,256]{2,1,0:T(8,128)(2,1)S(1)}, bf16[2,128,256]{2,1,0:T(8,128)(2,1)S(1)}, u32[]{:S(2)}, u32[]{:S(2)}) collective-permute-start(bf16[2,128,256]{2,1,0:T(8,128)(2,1)S(1)} %slice_bitcast_fusion), channel_id=1, source_target_pairs={{0,6},{1,7},{2,0},{3,1},{4,2},{5,3},{6,4},{7,5},{8,14},{9,15},{10,... | collective-permute-start | bytes 393224 | tf_op jit(solution)/shard_map/ppermute | solution.py:56
  30.3 1.5 %collective-permute-start.5 = (bf16[128,1792]{1,0:T(8,128)(2,1)S(1)}, bf16[128,1792]{1,0:T(8,128)(2,1)S(1)}, u32[]{:S(2)}, u32[]{:S(2)}) collective-permute-start(bf16[128,1792]{1,0:T(8,128)(2,1)S(1)} %slice.24), channel_id=1, source_target_pairs={{0,8},{8,16},{16,24},{24,0},{32,40},{40,48},{48,56},{56,32},{64,72... | collective-permute-start | bytes 1376264 | tf_op jit(solution)/shard_map/ppermute | solution.py:52
  33.0 3.4 %collective-permute-done.12 = bf16[2,128,256]{2,1,0:T(8,128)(2,1)S(1)} collective-permute-done((bf16[2,128,256]{2,1,0:T(8,128)(2,1)S(1)}, bf16[2,128,256]{2,1,0:T(8,128)(2,1)S(1)}, u32[]{:S(2)}, u32[]{:S(2)}) %collective-permute-start.12) | collective-permute-done | bytes 131104 | tf_op jit(solution)/shard_map/ppermute | solution.py:56
  36.4 6.9 %collective-permute-done.5.refs_2_ = bf16[128,1792]{1,0:T(8,128)(2,1)S(1)} collective-permute-done((bf16[128,1792]{1,0:T(8,128)(2,1)S(1)}, bf16[128,1792]{1,0:T(8,128)(2,1)S(1)}, u32[]{:S(2)}, u32[]{:S(2)}) %collective-permute-start.5) | collective-permute-done | bytes 458784 | tf_op jit(solution)/shard_map/ppermute | solution.py:52
  43.3 2.5 %collective-permute-done.6.refs_3_ = bf16[128,1792]{1,0:T(8,128)(2,1)S(1)} collective-permute-done((bf16[128,1792]{1,0:T(8,128)(2,1)S(1)}, bf16[128,1792]{1,0:T(8,128)(2,1)S(1)}, u32[]{:S(2)}, u32[]{:S(2)}) %collective-permute-start.6) | collective-permute-done | bytes 458784 | tf_op jit(solution)/shard_map/ppermute | solution.py:52
  47.5 2.3 %sent_sums.4 = bf16[2,1040,128]{2,1,0:T(8,128)(2,1)S(1)} custom-call(s32[32]{0:T(128)S(1)} %stack.103.slots, bf16[256,1792]{1,0:T(8,128)(2,1)S(1)} %copy-done, bf16[256,1792]{1,0:T(8,128)(2,1)S(1)} %collective-permute-done.3.refs_1_, bf16[128,1792]{1,0:T(8,128)(2,1)S(1)} %collective-permute-done.5.refs_2_, ...), custom_call_target="tpu_custom_call" | custom-call | flops 536870912 | bytes 1 | tf_op jit(solution)/shard_map/sent_sums/pallas_call | solution.py:154
  49.8 1.8 %collective-permute-start.14 = (bf16[2,1040,128]{2,1,0:T(8,128)(2,1)S(1)}, bf16[2,1040,128]{2,1,0:T(8,128)(2,1)S(1)}, u32[]{:S(2)}, u32[]{:S(2)}) collective-permute-start(bf16[2,1040,128]{2,1,0:T(8,128)(2,1)S(1)} %sent_sums.4), channel_id=1, source_target_pairs={{0,32},{8,40},{16,48},{24,56},{32,0},{40,8},{48,16},{56,24},{64,96... | collective-permute-start | bytes 1597448 | tf_op jit(solution)/shard_map/ppermute | solution.py:31
  51.6 2.3 %sent_sums.5 = bf16[2,1040,128]{2,1,0:T(8,128)(2,1)S(1)} custom-call(s32[32]{0:T(128)S(1)} %stack.103.slots, bf16[256,1792]{1,0:T(8,128)(2,1)S(1)} %copy-done, bf16[256,1792]{1,0:T(8,128)(2,1)S(1)} %collective-permute-done.3.refs_1_, bf16[128,1792]{1,0:T(8,128)(2,1)S(1)} %collective-permute-done.5.refs_2_, ...), custom_call_target="tpu_custom_call" | custom-call | flops 536870912 | bytes 1 | tf_op jit(solution)/shard_map/sent_sums/pallas_call | solution.py:154
  53.9 2.2 %collective-permute-start.15 = (bf16[2,1040,128]{2,1,0:T(8,128)(2,1)S(1)}, bf16[2,1040,128]{2,1,0:T(8,128)(2,1)S(1)}, u32[]{:S(2)}, u32[]{:S(2)}) collective-permute-start(bf16[2,1040,128]{2,1,0:T(8,128)(2,1)S(1)} %sent_sums.5), channel_id=1, source_target_pairs={{0,96},{8,104},{16,112},{24,120},{32,64},{40,72},{48,80},{56,88},{... | collective-permute-start | bytes 1597448 | tf_op jit(solution)/shard_map/ppermute | solution.py:31
  56.1 2.3 %sent_sums.6 = bf16[2,1040,128]{2,1,0:T(8,128)(2,1)S(1)} custom-call(s32[32]{0:T(128)S(1)} %stack.103.slots, bf16[256,1792]{1,0:T(8,128)(2,1)S(1)} %copy-done, bf16[256,1792]{1,0:T(8,128)(2,1)S(1)} %collective-permute-done.3.refs_1_, bf16[128,1792]{1,0:T(8,128)(2,1)S(1)} %collective-permute-done.5.refs_2_, ...), custom_call_target="tpu_custom_call" | custom-call | flops 536870912 | bytes 1 | tf_op jit(solution)/shard_map/sent_sums/pallas_call | solution.py:154
  58.4 1.7 %collective-permute-start.16 = (bf16[2,1040,128]{2,1,0:T(8,128)(2,1)S(1)}, bf16[2,1040,128]{2,1,0:T(8,128)(2,1)S(1)}, u32[]{:S(2)}, u32[]{:S(2)}) collective-permute-start(bf16[2,1040,128]{2,1,0:T(8,128)(2,1)S(1)} %sent_sums.6), channel_id=1, source_target_pairs={{0,128},{8,136},{16,144},{24,152},{32,160},{40,168},{48,176},{56,1... | collective-permute-start | bytes 1597448 | tf_op jit(solution)/shard_map/ppermute | solution.py:31
  62.1 2.2 %kept_sums.4.mine = f32[512,512]{1,0:T(8,128)S(1)} custom-call(s32[32]{0:T(128)S(1)} %stack.103.slots, bf16[256,1792]{1,0:T(8,128)(2,1)S(1)} %copy-done, bf16[256,1792]{1,0:T(8,128)(2,1)S(1)} %collective-permute-done.3.refs_1_, bf16[128,1792]{1,0:T(8,128)(2,1)S(1)} %collective-permute-done.5.refs_2_, bf16[128,1792]{1,0:T(8,128)(2,1)S(1)} %collective-permute-done.6.refs_3_, ...), custom_call_target="tpu_custom_call" | custom-call | flops 536870912 | bytes 1 | tf_op jit(solution)/shard_map/kept_sums/pallas_call | solution.py:154
  64.3 2.2 %kept_sums.5.mine = f32[512,512]{1,0:T(8,128)S(1)} custom-call(s32[32]{0:T(128)S(1)} %stack.103.slots, bf16[256,1792]{1,0:T(8,128)(2,1)S(1)} %copy-done, bf16[256,1792]{1,0:T(8,128)(2,1)S(1)} %collective-permute-done.3.refs_1_, bf16[128,1792]{1,0:T(8,128)(2,1)S(1)} %collective-permute-done.5.refs_2_, bf16[128,1792]{1,0:T(8,128)(2,1)S(1)} %collective-permute-done.6.refs_3_, ...), custom_call_target="tpu_custom_call" | custom-call | flops 536870912 | bytes 1 | tf_op jit(solution)/shard_map/kept_sums/pallas_call | solution.py:154
  69.0 2.2 %kept_sums.6.mine = f32[512,512]{1,0:T(8,128)S(1)} custom-call(s32[32]{0:T(128)S(1)} %stack.103.slots, bf16[256,1792]{1,0:T(8,128)(2,1)S(1)} %copy-done, bf16[256,1792]{1,0:T(8,128)(2,1)S(1)} %collective-permute-done.3.refs_1_, bf16[128,1792]{1,0:T(8,128)(2,1)S(1)} %collective-permute-done.5.refs_2_, bf16[128,1792]{1,0:T(8,128)(2,1)S(1)} %collective-permute-done.6.refs_3_, ...), custom_call_target="tpu_custom_call" | custom-call | flops 536870912 | bytes 1 | tf_op jit(solution)/shard_map/kept_sums/pallas_call | solution.py:154
  77.7 2.0 %collective-permute-start.21 = (bf16[1,528,128]{2,1,0:T(8,128)(2,1)S(1)}, bf16[1,528,128]{2,1,0:T(8,128)(2,1)S(1)}, u32[]{:S(2)}, u32[]{:S(2)}) collective-permute-start(bf16[1,528,128]{2,1,0:T(8,128)(2,1)S(1)} %get-tuple-element.67), channel_id=1, source_target_pairs={{0,96},{8,104},{16,112},{24,120},{32,64},{40,72},{48,80},{56,88},{... | collective-permute-start | bytes 405512 | tf_op jit(solution)/shard_map/ppermute | solution.py:31
  82.6 1.8 %collective-permute-start.24 = (bf16[2,272,128]{2,1,0:T(8,128)(2,1)S(1)}, bf16[2,272,128]{2,1,0:T(8,128)(2,1)S(1)}, u32[]{:S(2)}, u32[]{:S(2)}) collective-permute-start(bf16[2,272,128]{2,1,0:T(8,128)(2,1)S(1)} %get-tuple-element.71), channel_id=1, source_target_pairs={{0,128},{8,136},{16,144},{24,152},{32,160},{40,168},{48,176},{56,1... | collective-permute-start | bytes 417800 | tf_op jit(solution)/shard_map/ppermute | solution.py:31
  85.9 2.4 %collective-permute-start.23 = (bf16[2,272,128]{2,1,0:T(8,128)(2,1)S(1)}, bf16[2,272,128]{2,1,0:T(8,128)(2,1)S(1)}, u32[]{:S(2)}, u32[]{:S(2)}) collective-permute-start(bf16[2,272,128]{2,1,0:T(8,128)(2,1)S(1)} %get-tuple-element.70), channel_id=1, source_target_pairs={{0,96},{8,104},{16,112},{24,120},{32,64},{40,72},{48,80},{56,88},{... | collective-permute-start | bytes 417800 | tf_op jit(solution)/shard_map/ppermute | solution.py:31
  (71 shorter events, 28.5 us)
Async XLA Ops:
  1.1 6.9 %collective-permute-start.2 = (bf16[128,256]{1,0:T(8,128)(2,1)S(1)}, bf16[128,256]{1,0:T(8,128)(2,1)S(1)}, u32[]{:S(2)}, u32[]{:S(2)}) collective-permute-start(bf16[128,256]{1,0:T(8,128)(2,1)S(1)} %bitcast.38), channel_id=1, source_target_pairs={{0,8},{8,16},{16,24},{24,0},{32,40},{40,48},{48,56},{56,32},{64,72... | collective-permute-start | bytes 196616 | tf_op jit(solution)/shard_map/ppermute | solution.py:52
  3.2 5.7 %collective-permute-start = (bf16[128,256]{1,0:T(8,128)(2,1)S(1)}, bf16[128,256]{1,0:T(8,128)(2,1)S(1)}, u32[]{:S(2)}, u32[]{:S(2)}) collective-permute-start(bf16[128,256]{1,0:T(8,128)(2,1)S(1)} %bitcast.39), channel_id=1, source_target_pairs={{0,24},{8,0},{16,8},{24,16},{32,56},{40,32},{48,40},{56,48},{64,88... | collective-permute-start | bytes 196616 | tf_op jit(solution)/shard_map/ppermute | solution.py:52
  3.5 6.6 %collective-permute-start.1 = (bf16[128,256]{1,0:T(8,128)(2,1)S(1)}, bf16[128,256]{1,0:T(8,128)(2,1)S(1)}, u32[]{:S(2)}, u32[]{:S(2)}) collective-permute-start(bf16[128,256]{1,0:T(8,128)(2,1)S(1)} %bitcast.40), channel_id=1, source_target_pairs={{0,16},{8,24},{16,0},{24,8},{32,48},{40,56},{48,32},{56,40},{64,80... | collective-permute-start | bytes 196616 | tf_op jit(solution)/shard_map/ppermute | solution.py:52
  5.0 25.2 %collective-permute-start.4 = (bf16[256,1792]{1,0:T(8,128)(2,1)}, bf16[256,1792]{1,0:T(8,128)(2,1)S(1)}, u32[]{:S(2)}, u32[]{:S(2)}) collective-permute-start(bf16[256,1792]{1,0:T(8,128)(2,1)} %refs_0_.15), channel_id=1, source_target_pairs={{0,8},{8,16},{16,24},{24,0},{32,40},{40,48},{48,56},{56,32},{64,72... | collective-permute-start | bytes 2752520 | tf_op jit(solution)/shard_map/ppermute | solution.py:52
  7.0 23.3 %collective-permute-start.3 = (bf16[256,1792]{1,0:T(8,128)(2,1)}, bf16[256,1792]{1,0:T(8,128)(2,1)S(1)}, u32[]{:S(2)}, u32[]{:S(2)}) collective-permute-start(bf16[256,1792]{1,0:T(8,128)(2,1)} %refs_0_.15), channel_id=1, source_target_pairs={{0,24},{8,0},{16,8},{24,16},{32,56},{40,32},{48,40},{56,48},{64,88... | collective-permute-start | bytes 2752520 | tf_op jit(solution)/shard_map/ppermute | solution.py:52
  10.1 12.4 %collective-permute-start.9 = (bf16[4,128,256]{2,1,0:T(8,128)(2,1)S(1)}, bf16[4,128,256]{2,1,0:T(8,128)(2,1)S(1)}, u32[]{:S(2)}, u32[]{:S(2)}) collective-permute-start(bf16[4,128,256]{2,1,0:T(8,128)(2,1)S(1)} %pad_maximum_fusion.1), channel_id=1, source_target_pairs={{0,2},{1,3},{2,4},{3,5},{4,6},{5,7},{6,0},{7,1},{8,10},{9,11},{10,... | collective-permute-start | bytes 786440 | tf_op jit(solution)/shard_map/ppermute | solution.py:56
  13.4 14.3 %collective-permute-start.8 = (bf16[4,128,256]{2,1,0:T(8,128)(2,1)S(1)}, bf16[4,128,256]{2,1,0:T(8,128)(2,1)S(1)}, u32[]{:S(2)}, u32[]{:S(2)}) collective-permute-start(bf16[4,128,256]{2,1,0:T(8,128)(2,1)S(1)} %pad_maximum_fusion.1), channel_id=1, source_target_pairs={{0,6},{1,7},{2,0},{3,1},{4,2},{5,3},{6,4},{7,5},{8,14},{9,15},{10,... | collective-permute-start | bytes 786440 | tf_op jit(solution)/shard_map/ppermute | solution.py:56
  16.5 15.4 %collective-permute-start.7 = (bf16[4,128,256]{2,1,0:T(8,128)(2,1)S(1)}, bf16[4,128,256]{2,1,0:T(8,128)(2,1)S(1)}, u32[]{:S(2)}, u32[]{:S(2)}) collective-permute-start(bf16[4,128,256]{2,1,0:T(8,128)(2,1)S(1)} %pad_maximum_fusion.1), channel_id=1, source_target_pairs={{0,1},{1,0},{2,3},{3,2},{4,5},{5,4},{6,7},{7,6},{8,9},{9,8},{10,11... | collective-permute-start | bytes 786440 | tf_op jit(solution)/shard_map/ppermute | solution.py:60
  22.5 10.5 %collective-permute-start.11 = (bf16[2,128,256]{2,1,0:T(8,128)(2,1)S(1)}, bf16[2,128,256]{2,1,0:T(8,128)(2,1)S(1)}, u32[]{:S(2)}, u32[]{:S(2)}) collective-permute-start(bf16[2,128,256]{2,1,0:T(8,128)(2,1)S(1)} %slice_bitcast_fusion.1), channel_id=1, source_target_pairs={{0,2},{1,3},{2,4},{3,5},{4,6},{5,7},{6,0},{7,1},{8,10},{9,11},{10,... | collective-permute-start | bytes 393224 | tf_op jit(solution)/shard_map/ppermute | solution.py:56
  27.8 8.6 %collective-permute-start.12 = (bf16[2,128,256]{2,1,0:T(8,128)(2,1)S(1)}, bf16[2,128,256]{2,1,0:T(8,128)(2,1)S(1)}, u32[]{:S(2)}, u32[]{:S(2)}) collective-permute-start(bf16[2,128,256]{2,1,0:T(8,128)(2,1)S(1)} %slice_bitcast_fusion), channel_id=1, source_target_pairs={{0,6},{1,7},{2,0},{3,1},{4,2},{5,3},{6,4},{7,5},{8,14},{9,15},{10,... | collective-permute-start | bytes 393224 | tf_op jit(solution)/shard_map/ppermute | solution.py:56
  30.2 15.7 %collective-permute-start.10 = (bf16[2,4,128,256]{3,2,1,0:T(8,128)(2,1)S(1)}, bf16[2,4,128,256]{3,2,1,0:T(8,128)(2,1)S(1)}, u32[]{:S(2)}, u32[]{:S(2)}) collective-permute-start(bf16[2,4,128,256]{3,2,1,0:T(8,128)(2,1)S(1)} %pad_maximum_fusion), channel_id=1, source_target_pairs={{0,1},{1,0},{2,3},{3,2},{4,5},{5,4},{6,7},{7,6},{8,9},{9,8},{10,11... | collective-permute-start | bytes 1572872 | tf_op jit(solution)/shard_map/ppermute | solution.py:60
  30.3 13.0 %collective-permute-start.5 = (bf16[128,1792]{1,0:T(8,128)(2,1)S(1)}, bf16[128,1792]{1,0:T(8,128)(2,1)S(1)}, u32[]{:S(2)}, u32[]{:S(2)}) collective-permute-start(bf16[128,1792]{1,0:T(8,128)(2,1)S(1)} %slice.24), channel_id=1, source_target_pairs={{0,8},{8,16},{16,24},{24,0},{32,40},{40,48},{48,56},{56,32},{64,72... | collective-permute-start | bytes 1376264 | tf_op jit(solution)/shard_map/ppermute | solution.py:52
  31.9 13.9 %collective-permute-start.6 = (bf16[128,1792]{1,0:T(8,128)(2,1)S(1)}, bf16[128,1792]{1,0:T(8,128)(2,1)S(1)}, u32[]{:S(2)}, u32[]{:S(2)}) collective-permute-start(bf16[128,1792]{1,0:T(8,128)(2,1)S(1)} %slice.25), channel_id=1, source_target_pairs={{0,24},{8,0},{16,8},{24,16},{32,56},{40,32},{48,40},{56,48},{64,88... | collective-permute-start | bytes 1376264 | tf_op jit(solution)/shard_map/ppermute | solution.py:52
  49.8 16.7 %collective-permute-start.14 = (bf16[2,1040,128]{2,1,0:T(8,128)(2,1)S(1)}, bf16[2,1040,128]{2,1,0:T(8,128)(2,1)S(1)}, u32[]{:S(2)}, u32[]{:S(2)}) collective-permute-start(bf16[2,1040,128]{2,1,0:T(8,128)(2,1)S(1)} %sent_sums.4), channel_id=1, source_target_pairs={{0,32},{8,40},{16,48},{24,56},{32,0},{40,8},{48,16},{56,24},{64,96... | collective-permute-start | bytes 1597448 | tf_op jit(solution)/shard_map/ppermute | solution.py:31
  53.9 17.3 %collective-permute-start.15 = (bf16[2,1040,128]{2,1,0:T(8,128)(2,1)S(1)}, bf16[2,1040,128]{2,1,0:T(8,128)(2,1)S(1)}, u32[]{:S(2)}, u32[]{:S(2)}) collective-permute-start(bf16[2,1040,128]{2,1,0:T(8,128)(2,1)S(1)} %sent_sums.5), channel_id=1, source_target_pairs={{0,96},{8,104},{16,112},{24,120},{32,64},{40,72},{48,80},{56,88},{... | collective-permute-start | bytes 1597448 | tf_op jit(solution)/shard_map/ppermute | solution.py:31
  58.4 16.0 %collective-permute-start.16 = (bf16[2,1040,128]{2,1,0:T(8,128)(2,1)S(1)}, bf16[2,1040,128]{2,1,0:T(8,128)(2,1)S(1)}, u32[]{:S(2)}, u32[]{:S(2)}) collective-permute-start(bf16[2,1040,128]{2,1,0:T(8,128)(2,1)S(1)} %sent_sums.6), channel_id=1, source_target_pairs={{0,128},{8,136},{16,144},{24,152},{32,160},{40,168},{48,176},{56,1... | collective-permute-start | bytes 1597448 | tf_op jit(solution)/shard_map/ppermute | solution.py:31
  61.4 15.5 %collective-permute-start.17 = (bf16[1,1040,128]{2,1,0:T(8,128)(2,1)S(1)}, bf16[1,1040,128]{2,1,0:T(8,128)(2,1)S(1)}, u32[]{:S(2)}, u32[]{:S(2)}) collective-permute-start(bf16[1,1040,128]{2,1,0:T(8,128)(2,1)S(1)} %sent_sums.7), channel_id=1, source_target_pairs={{0,32},{8,40},{16,48},{24,56},{32,0},{40,8},{48,16},{56,24},{64,96... | collective-permute-start | bytes 798728 | tf_op jit(solution)/shard_map/ppermute | solution.py:31
  67.6 12.1 %collective-permute-start.18 = (bf16[2,528,128]{2,1,0:T(8,128)(2,1)S(1)}, bf16[2,528,128]{2,1,0:T(8,128)(2,1)S(1)}, u32[]{:S(2)}, u32[]{:S(2)}) collective-permute-start(bf16[2,528,128]{2,1,0:T(8,128)(2,1)S(1)} %get-tuple-element.58), channel_id=1, source_target_pairs={{0,96},{8,104},{16,112},{24,120},{32,64},{40,72},{48,80},{56,88},{... | collective-permute-start | bytes 811016 | tf_op jit(solution)/shard_map/ppermute | solution.py:31
  72.4 9.4 %collective-permute-start.19 = (bf16[2,528,128]{2,1,0:T(8,128)(2,1)S(1)}, bf16[2,528,128]{2,1,0:T(8,128)(2,1)S(1)}, u32[]{:S(2)}, u32[]{:S(2)}) collective-permute-start(bf16[2,528,128]{2,1,0:T(8,128)(2,1)S(1)} %get-tuple-element.61), channel_id=1, source_target_pairs={{0,32},{8,40},{16,48},{24,56},{32,0},{40,8},{48,16},{56,24},{64,96... | collective-permute-start | bytes 811016 | tf_op jit(solution)/shard_map/ppermute | solution.py:31
  75.5 9.4 %collective-permute-start.20 = (bf16[2,528,128]{2,1,0:T(8,128)(2,1)S(1)}, bf16[2,528,128]{2,1,0:T(8,128)(2,1)S(1)}, u32[]{:S(2)}, u32[]{:S(2)}) collective-permute-start(bf16[2,528,128]{2,1,0:T(8,128)(2,1)S(1)} %get-tuple-element.64), channel_id=1, source_target_pairs={{0,32},{8,40},{16,48},{24,56},{32,0},{40,8},{48,16},{56,24},{64,96... | collective-permute-start | bytes 811016 | tf_op jit(solution)/shard_map/ppermute | solution.py:31
  77.7 10.6 %collective-permute-start.21 = (bf16[1,528,128]{2,1,0:T(8,128)(2,1)S(1)}, bf16[1,528,128]{2,1,0:T(8,128)(2,1)S(1)}, u32[]{:S(2)}, u32[]{:S(2)}) collective-permute-start(bf16[1,528,128]{2,1,0:T(8,128)(2,1)S(1)} %get-tuple-element.67), channel_id=1, source_target_pairs={{0,96},{8,104},{16,112},{24,120},{32,64},{40,72},{48,80},{56,88},{... | collective-permute-start | bytes 405512 | tf_op jit(solution)/shard_map/ppermute | solution.py:31
  80.7 8.8 %collective-permute-start.25 = (bf16[2,272,128]{2,1,0:T(8,128)(2,1)S(1)}, bf16[2,272,128]{2,1,0:T(8,128)(2,1)S(1)}, u32[]{:S(2)}, u32[]{:S(2)}) collective-permute-start(bf16[2,272,128]{2,1,0:T(8,128)(2,1)S(1)} %get-tuple-element.72), channel_id=1, source_target_pairs={{0,128},{8,136},{16,144},{24,152},{32,160},{40,168},{48,176},{56,1... | collective-permute-start | bytes 417800 | tf_op jit(solution)/shard_map/ppermute | solution.py:31
  82.6 7.8 %collective-permute-start.24 = (bf16[2,272,128]{2,1,0:T(8,128)(2,1)S(1)}, bf16[2,272,128]{2,1,0:T(8,128)(2,1)S(1)}, u32[]{:S(2)}, u32[]{:S(2)}) collective-permute-start(bf16[2,272,128]{2,1,0:T(8,128)(2,1)S(1)} %get-tuple-element.71), channel_id=1, source_target_pairs={{0,128},{8,136},{16,144},{24,152},{32,160},{40,168},{48,176},{56,1... | collective-permute-start | bytes 417800 | tf_op jit(solution)/shard_map/ppermute | solution.py:31
  85.9 6.4 %collective-permute-start.23 = (bf16[2,272,128]{2,1,0:T(8,128)(2,1)S(1)}, bf16[2,272,128]{2,1,0:T(8,128)(2,1)S(1)}, u32[]{:S(2)}, u32[]{:S(2)}) collective-permute-start(bf16[2,272,128]{2,1,0:T(8,128)(2,1)S(1)} %get-tuple-element.70), channel_id=1, source_target_pairs={{0,96},{8,104},{16,112},{24,120},{32,64},{40,72},{48,80},{56,88},{... | collective-permute-start | bytes 417800 | tf_op jit(solution)/shard_map/ppermute | solution.py:31
  (3 other events, 21.5 us)

commit v4 on v3

--- a/solution.py
+++ b/solution.py
@@ -64,7 +64,7 @@
     return lax.optimization_barrier((later, *earlier))[0]
 
 
-def put(ref, parts):
+def put(ref, parts, tile=0):
     pieces = [p[:, n : n + LANES] for p in parts for n in range(0, TILE, LANES)]
     tops = [jnp.max(p, axis=0, keepdims=True) for p in pieces]
     top = functools.reduce(jnp.maximum, tops)
@@ -76,16 +76,16 @@
         scaled = scaled * scaled
         scaled = scaled * scaled
         scaled = scaled * scaled
-        ref[0, row : row + piece.shape[0], :] = scaled.astype(jnp.bfloat16)
+        ref[tile, row : row + piece.shape[0], :] = scaled.astype(jnp.bfloat16)
         row += piece.shape[0]
-    ref[0, row:, :] = jnp.broadcast_to(top, (16, LANES)).astype(jnp.bfloat16)
-
-
-def get(ref, start, rows):
-    scale = ref[0, -16:, :].astype(jnp.float32)[:1] * (1.0 / CODE_TOP)
+    ref[tile, row:, :] = jnp.broadcast_to(top, (16, LANES)).astype(jnp.bfloat16)
+
+
+def get(ref, start, rows, tile=0):
+    scale = ref[tile, -16:, :].astype(jnp.float32)[:1] * (1.0 / CODE_TOP)
     found = []
     for n in range(TILE // LANES):
-        code = ref[0, start + n * rows : start + (n + 1) * rows, :]
+        code = ref[tile, start + n * rows : start + (n + 1) * rows, :]
         value = jnp.maximum(code.astype(jnp.float32), 2.0**-126)
         found.append(jnp.exp(jnp.log(value) * 0.125) * scale)
     return jnp.concatenate(found, axis=1)
@@ -131,13 +131,16 @@
 def fold_kernel(slots, mine, received, kept, sent):
     half = kept.shape[0] // LEN
     rows = LEN * (TILE // LANES)
-
-    def block(n):
-        return mine[n * LEN : (n + 1) * LEN, :] + get(received, n * rows, LEN)
-
-    put(sent, [block(n) for n in range(half, 2 * half)])
-    for n in range(half):
-        kept[n * LEN : (n + 1) * LEN, :] = block(n)
+    for tile in range(kept.shape[1] // TILE):
+        at = slice(tile * TILE, (tile + 1) * TILE)
+
+        def block(n):
+            own = mine[n * LEN : (n + 1) * LEN, at]
+            return own + get(received, n * rows, LEN, tile)
+
+        put(sent, [block(n) for n in range(half, 2 * half)], tile)
+        for n in range(half):
+            kept[n * LEN : (n + 1) * LEN, at] = block(n)
 
 
 def final_kernel(mine, received, *refs):
@@ -191,13 +194,25 @@
     return sums(kept_kernel, "kept_sums", run, slots, acts, grads, start, out)
 
 
+def held(array):
+    return pltpu.with_memory_space_constraint(array, pltpu.VMEM)
+
+
 def fold(slots, mine, received):
     rows, features = mine.shape[0] // 2, mine.shape[1]
-    outs = (
-        ((rows, features), jnp.float32),
-        (message(rows, features), jnp.bfloat16),
-    )
-    return call(fold_kernel, "fold", features, slots, [(mine, 0), (received, 0)], outs, 1)
+    space = pl.BlockSpec(memory_space=pltpu.VMEM)
+    return pl.pallas_call(
+        fold_kernel,
+        name="fold",
+        in_specs=[pl.BlockSpec(memory_space=pltpu.SMEM), space, space],
+        out_specs=[space, space],
+        out_shape=[
+            pltpu.VMEM((rows, features), jnp.float32),
+            pltpu.VMEM(message(rows, features), jnp.bfloat16),
+        ],
+        compiler_params=pltpu.CompilerParams(vmem_limit_bytes=VMEM),
+        cost_estimate=pl.CostEstimate(flops=1, bytes_accessed=1, transcendentals=0),
+    )(slots, held(mine), held(received))
 
 
 def final(mine, received, start, total, before):

time: 94.3 us -> 93.8 us (level)
    pallas_call x16 -> x8, Pallas kernels: 23.6 us -> 16.1 us  [call(): pl.pallas_call(body, name=name, grid_spec=pltpu.PrefetchScalarGridSpec(nu...]
    pallas_call x0 -> x8, Pallas kernels: none -> 6.66 us  [fold(): pl.pallas_call(fold_kernel, name='fold', in_specs=[pl.BlockSpec(memory_sp...]
  transfers between devices with their start and end apart: 26 -> 26, of which waited for: 12 -> 12; matrix products, arithmetic and copies ran while one was open for 1% -> 1% of each run, Pallas kernels for 26% -> 25%
where the time goes in v4:
time: 93.8 us; the launch traced here: 93.7 us
  starting transfers between devices  39.9 us (43%)
  Pallas kernels  26.4 us (28%)
  waiting for transfers between devices  25.1 us (27%)
  local copies, waits for them, and re-layouts  1.73 us (2%)
    ppermute x12, starting transfers between devices, swap(): return lax.ppermute(array, 'dp', pairs)  17.3 us
    pallas_call x8, Pallas kernels, call(): pl.pallas_call(body, name=name, grid_spec=pltpu.PrefetchScalarGridSpec(nu...  16.1 us
    ppermute x4, starting transfers between devices, from_z(): return lax.ppermute(array, 'tensor', tensor_moves(-offset, 0))  14.1 us
    ppermute x7, waiting for transfers between devices, from_y(): return lax.ppermute(array, 'dp', pairs)  11.6 us
    ppermute x4, waiting for transfers between devices, from_z(): return lax.ppermute(array, 'tensor', tensor_moves(-offset, 0))  9.64 us
    ppermute x7, starting transfers between devices, from_y(): return lax.ppermute(array, 'dp', pairs)  8.48 us
    pallas_call x8, Pallas kernels, fold(): pl.pallas_call(fold_kernel, name='fold', in_specs=[pl.BlockSpec(memory_sp...  6.66 us
    pallas_call x4, Pallas kernels, final(): pl.pallas_call(final_kernel, name='final', grid=(mine.shape[1] // TILE,),...  3.65 us
  transfers between devices with their start and end apart: 26, of which 12 were waited for; matrix products, arithmetic and copies ran while one was open for 1% of the time, Pallas kernels for 25%

profile of v4, /device:TPU:24, one launch (start us, length us, event | category | flops | bytes accessed | tf_op | source)
XLA Modules:
  0.0 93.7 jit_solution(5336602348359494777)
XLA Ops:
  1.1 2.0 %collective-permute-start.2 = (bf16[128,256]{1,0:T(8,128)(2,1)S(1)}, bf16[128,256]{1,0:T(8,128)(2,1)S(1)}, u32[]{:S(2)}, u32[]{:S(2)}) collective-permute-start(bf16[128,256]{1,0:T(8,128)(2,1)S(1)} %bitcast.38), channel_id=1, source_target_pairs={{0,8},{8,16},{16,24},{24,0},{32,40},{40,48},{48,56},{56,32},{64,72... | collective-permute-start | bytes 196616 | tf_op jit(solution)/shard_map/ppermute | solution.py:52
  3.5 1.5 %collective-permute-start.1 = (bf16[128,256]{1,0:T(8,128)(2,1)S(1)}, bf16[128,256]{1,0:T(8,128)(2,1)S(1)}, u32[]{:S(2)}, u32[]{:S(2)}) collective-permute-start(bf16[128,256]{1,0:T(8,128)(2,1)S(1)} %bitcast.40), channel_id=1, source_target_pairs={{0,16},{8,24},{16,0},{24,8},{32,48},{40,56},{48,32},{56,40},{64,80... | collective-permute-start | bytes 196616 | tf_op jit(solution)/shard_map/ppermute | solution.py:52
  5.0 2.0 %collective-permute-start.4 = (bf16[256,1792]{1,0:T(8,128)(2,1)}, bf16[256,1792]{1,0:T(8,128)(2,1)S(1)}, u32[]{:S(2)}, u32[]{:S(2)}) collective-permute-start(bf16[256,1792]{1,0:T(8,128)(2,1)} %refs_0_.15), channel_id=1, source_target_pairs={{0,8},{8,16},{16,24},{24,0},{32,40},{40,48},{48,56},{56,32},{64,72... | collective-permute-start | bytes 2752520 | tf_op jit(solution)/shard_map/ppermute | solution.py:52
  10.1 3.3 %collective-permute-start.9 = (bf16[4,128,256]{2,1,0:T(8,128)(2,1)S(1)}, bf16[4,128,256]{2,1,0:T(8,128)(2,1)S(1)}, u32[]{:S(2)}, u32[]{:S(2)}) collective-permute-start(bf16[4,128,256]{2,1,0:T(8,128)(2,1)S(1)} %pad_maximum_fusion.1), channel_id=1, source_target_pairs={{0,2},{1,3},{2,4},{3,5},{4,6},{5,7},{6,0},{7,1},{8,10},{9,11},{10,... | collective-permute-start | bytes 786440 | tf_op jit(solution)/shard_map/ppermute | solution.py:56
  13.4 3.1 %collective-permute-start.8 = (bf16[4,128,256]{2,1,0:T(8,128)(2,1)S(1)}, bf16[4,128,256]{2,1,0:T(8,128)(2,1)S(1)}, u32[]{:S(2)}, u32[]{:S(2)}) collective-permute-start(bf16[4,128,256]{2,1,0:T(8,128)(2,1)S(1)} %pad_maximum_fusion.1), channel_id=1, source_target_pairs={{0,6},{1,7},{2,0},{3,1},{4,2},{5,3},{6,4},{7,5},{8,14},{9,15},{10,... | collective-permute-start | bytes 786440 | tf_op jit(solution)/shard_map/ppermute | solution.py:56
  16.6 5.9 %collective-permute-done.9 = bf16[4,128,256]{2,1,0:T(8,128)(2,1)S(1)} collective-permute-done((bf16[4,128,256]{2,1,0:T(8,128)(2,1)S(1)}, bf16[4,128,256]{2,1,0:T(8,128)(2,1)S(1)}, u32[]{:S(2)}, u32[]{:S(2)}) %collective-permute-start.9) | collective-permute-done | bytes 262176 | tf_op jit(solution)/shard_map/ppermute | solution.py:56
  22.5 5.3 %collective-permute-start.11 = (bf16[2,128,256]{2,1,0:T(8,128)(2,1)S(1)}, bf16[2,128,256]{2,1,0:T(8,128)(2,1)S(1)}, u32[]{:S(2)}, u32[]{:S(2)}) collective-permute-start(bf16[2,128,256]{2,1,0:T(8,128)(2,1)S(1)} %slice_bitcast_fusion.1), channel_id=1, source_target_pairs={{0,2},{1,3},{2,4},{3,5},{4,6},{5,7},{6,0},{7,1},{8,10},{9,11},{10,... | collective-permute-start | bytes 393224 | tf_op jit(solution)/shard_map/ppermute | solution.py:56
  27.8 2.3 %collective-permute-start.12 = (bf16[2,128,256]{2,1,0:T(8,128)(2,1)S(1)}, bf16[2,128,256]{2,1,0:T(8,128)(2,1)S(1)}, u32[]{:S(2)}, u32[]{:S(2)}) collective-permute-start(bf16[2,128,256]{2,1,0:T(8,128)(2,1)S(1)} %slice_bitcast_fusion), channel_id=1, source_target_pairs={{0,6},{1,7},{2,0},{3,1},{4,2},{5,3},{6,4},{7,5},{8,14},{9,15},{10,... | collective-permute-start | bytes 393224 | tf_op jit(solution)/shard_map/ppermute | solution.py:56
  30.3 1.5 %collective-permute-start.5 = (bf16[128,1792]{1,0:T(8,128)(2,1)S(1)}, bf16[128,1792]{1,0:T(8,128)(2,1)S(1)}, u32[]{:S(2)}, u32[]{:S(2)}) collective-permute-start(bf16[128,1792]{1,0:T(8,128)(2,1)S(1)} %slice.24), channel_id=1, source_target_pairs={{0,8},{8,16},{16,24},{24,0},{32,40},{40,48},{48,56},{56,32},{64,72... | collective-permute-start | bytes 1376264 | tf_op jit(solution)/shard_map/ppermute | solution.py:52
  33.0 3.4 %collective-permute-done.12 = bf16[2,128,256]{2,1,0:T(8,128)(2,1)S(1)} collective-permute-done((bf16[2,128,256]{2,1,0:T(8,128)(2,1)S(1)}, bf16[2,128,256]{2,1,0:T(8,128)(2,1)S(1)}, u32[]{:S(2)}, u32[]{:S(2)}) %collective-permute-start.12) | collective-permute-done | bytes 131104 | tf_op jit(solution)/shard_map/ppermute | solution.py:56
  36.4 6.9 %collective-permute-done.5.refs_2_ = bf16[128,1792]{1,0:T(8,128)(2,1)S(1)} collective-permute-done((bf16[128,1792]{1,0:T(8,128)(2,1)S(1)}, bf16[128,1792]{1,0:T(8,128)(2,1)S(1)}, u32[]{:S(2)}, u32[]{:S(2)}) %collective-permute-start.5) | collective-permute-done | bytes 458784 | tf_op jit(solution)/shard_map/ppermute | solution.py:52
  43.3 2.5 %collective-permute-done.6.refs_3_ = bf16[128,1792]{1,0:T(8,128)(2,1)S(1)} collective-permute-done((bf16[128,1792]{1,0:T(8,128)(2,1)S(1)}, bf16[128,1792]{1,0:T(8,128)(2,1)S(1)}, u32[]{:S(2)}, u32[]{:S(2)}) %collective-permute-start.6) | collective-permute-done | bytes 458784 | tf_op jit(solution)/shard_map/ppermute | solution.py:52
  47.5 2.3 %sent_sums.4 = bf16[2,1040,128]{2,1,0:T(8,128)(2,1)S(1)} custom-call(s32[32]{0:T(128)S(1)} %stack.103.slots, bf16[256,1792]{1,0:T(8,128)(2,1)S(1)} %copy-done, bf16[256,1792]{1,0:T(8,128)(2,1)S(1)} %collective-permute-done.3.refs_1_, bf16[128,1792]{1,0:T(8,128)(2,1)S(1)} %collective-permute-done.5.refs_2_, ...), custom_call_target="tpu_custom_call" | custom-call | flops 536870912 | bytes 1 | tf_op jit(solution)/shard_map/sent_sums/pallas_call | solution.py:157
  49.8 1.8 %collective-permute-start.14 = (bf16[2,1040,128]{2,1,0:T(8,128)(2,1)S(1)}, bf16[2,1040,128]{2,1,0:T(8,128)(2,1)S(1)}, u32[]{:S(2)}, u32[]{:S(2)}) collective-permute-start(bf16[2,1040,128]{2,1,0:T(8,128)(2,1)S(1)} %sent_sums.4), channel_id=1, source_target_pairs={{0,32},{8,40},{16,48},{24,56},{32,0},{40,8},{48,16},{56,24},{64,96... | collective-permute-start | bytes 1597448 | tf_op jit(solution)/shard_map/ppermute | solution.py:31
  51.6 2.3 %sent_sums.5 = bf16[2,1040,128]{2,1,0:T(8,128)(2,1)S(1)} custom-call(s32[32]{0:T(128)S(1)} %stack.103.slots, bf16[256,1792]{1,0:T(8,128)(2,1)S(1)} %copy-done, bf16[256,1792]{1,0:T(8,128)(2,1)S(1)} %collective-permute-done.3.refs_1_, bf16[128,1792]{1,0:T(8,128)(2,1)S(1)} %collective-permute-done.5.refs_2_, ...), custom_call_target="tpu_custom_call" | custom-call | flops 536870912 | bytes 1 | tf_op jit(solution)/shard_map/sent_sums/pallas_call | solution.py:157
  53.9 2.2 %collective-permute-start.15 = (bf16[2,1040,128]{2,1,0:T(8,128)(2,1)S(1)}, bf16[2,1040,128]{2,1,0:T(8,128)(2,1)S(1)}, u32[]{:S(2)}, u32[]{:S(2)}) collective-permute-start(bf16[2,1040,128]{2,1,0:T(8,128)(2,1)S(1)} %sent_sums.5), channel_id=1, source_target_pairs={{0,96},{8,104},{16,112},{24,120},{32,64},{40,72},{48,80},{56,88},{... | collective-permute-start | bytes 1597448 | tf_op jit(solution)/shard_map/ppermute | solution.py:31
  56.1 2.3 %sent_sums.6 = bf16[2,1040,128]{2,1,0:T(8,128)(2,1)S(1)} custom-call(s32[32]{0:T(128)S(1)} %stack.103.slots, bf16[256,1792]{1,0:T(8,128)(2,1)S(1)} %copy-done, bf16[256,1792]{1,0:T(8,128)(2,1)S(1)} %collective-permute-done.3.refs_1_, bf16[128,1792]{1,0:T(8,128)(2,1)S(1)} %collective-permute-done.5.refs_2_, ...), custom_call_target="tpu_custom_call" | custom-call | flops 536870912 | bytes 1 | tf_op jit(solution)/shard_map/sent_sums/pallas_call | solution.py:157
  58.4 1.7 %collective-permute-start.16 = (bf16[2,1040,128]{2,1,0:T(8,128)(2,1)S(1)}, bf16[2,1040,128]{2,1,0:T(8,128)(2,1)S(1)}, u32[]{:S(2)}, u32[]{:S(2)}) collective-permute-start(bf16[2,1040,128]{2,1,0:T(8,128)(2,1)S(1)} %sent_sums.6), channel_id=1, source_target_pairs={{0,128},{8,136},{16,144},{24,152},{32,160},{40,168},{48,176},{56,1... | collective-permute-start | bytes 1597448 | tf_op jit(solution)/shard_map/ppermute | solution.py:31
  62.1 2.2 %kept_sums.4.mine = f32[512,512]{1,0:T(8,128)S(1)} custom-call(s32[32]{0:T(128)S(1)} %stack.103.slots, bf16[256,1792]{1,0:T(8,128)(2,1)S(1)} %copy-done, bf16[256,1792]{1,0:T(8,128)(2,1)S(1)} %collective-permute-done.3.refs_1_, bf16[128,1792]{1,0:T(8,128)(2,1)S(1)} %collective-permute-done.5.refs_2_, bf16[128,1792]{1,0:T(8,128)(2,1)S(1)} %collective-permute-done.6.refs_3_, ...), custom_call_target="tpu_custom_call" | custom-call | flops 536870912 | bytes 1 | tf_op jit(solution)/shard_map/kept_sums/pallas_call | solution.py:157
  64.3 2.2 %kept_sums.5.mine = f32[512,512]{1,0:T(8,128)S(1)} custom-call(s32[32]{0:T(128)S(1)} %stack.103.slots, bf16[256,1792]{1,0:T(8,128)(2,1)S(1)} %copy-done, bf16[256,1792]{1,0:T(8,128)(2,1)S(1)} %collective-permute-done.3.refs_1_, bf16[128,1792]{1,0:T(8,128)(2,1)S(1)} %collective-permute-done.5.refs_2_, bf16[128,1792]{1,0:T(8,128)(2,1)S(1)} %collective-permute-done.6.refs_3_, ...), custom_call_target="tpu_custom_call" | custom-call | flops 536870912 | bytes 1 | tf_op jit(solution)/shard_map/kept_sums/pallas_call | solution.py:157
  68.8 2.2 %kept_sums.6.mine = f32[512,512]{1,0:T(8,128)S(1)} custom-call(s32[32]{0:T(128)S(1)} %stack.103.slots, bf16[256,1792]{1,0:T(8,128)(2,1)S(1)} %copy-done, bf16[256,1792]{1,0:T(8,128)(2,1)S(1)} %collective-permute-done.3.refs_1_, bf16[128,1792]{1,0:T(8,128)(2,1)S(1)} %collective-permute-done.5.refs_2_, bf16[128,1792]{1,0:T(8,128)(2,1)S(1)} %collective-permute-done.6.refs_3_, ...), custom_call_target="tpu_custom_call" | custom-call | flops 536870912 | bytes 1 | tf_op jit(solution)/shard_map/kept_sums/pallas_call | solution.py:157
  77.2 2.0 %collective-permute-start.21 = (bf16[1,528,128]{2,1,0:T(8,128)(2,1)S(1)}, bf16[1,528,128]{2,1,0:T(8,128)(2,1)S(1)}, u32[]{:S(2)}, u32[]{:S(2)}) collective-permute-start(bf16[1,528,128]{2,1,0:T(8,128)(2,1)S(1)} %get-tuple-element.67), channel_id=1, source_target_pairs={{0,96},{8,104},{16,112},{24,120},{32,64},{40,72},{48,80},{56,88},{... | collective-permute-start | bytes 405512 | tf_op jit(solution)/shard_map/ppermute | solution.py:31
  82.3 1.7 %collective-permute-start.24 = (bf16[2,272,128]{2,1,0:T(8,128)(2,1)S(1)}, bf16[2,272,128]{2,1,0:T(8,128)(2,1)S(1)}, u32[]{:S(2)}, u32[]{:S(2)}) collective-permute-start(bf16[2,272,128]{2,1,0:T(8,128)(2,1)S(1)} %get-tuple-element.71), channel_id=1, source_target_pairs={{0,128},{8,136},{16,144},{24,152},{32,160},{40,168},{48,176},{56,1... | collective-permute-start | bytes 417800 | tf_op jit(solution)/shard_map/ppermute | solution.py:31
  85.4 2.4 %collective-permute-start.23 = (bf16[2,272,128]{2,1,0:T(8,128)(2,1)S(1)}, bf16[2,272,128]{2,1,0:T(8,128)(2,1)S(1)}, u32[]{:S(2)}, u32[]{:S(2)}) collective-permute-start(bf16[2,272,128]{2,1,0:T(8,128)(2,1)S(1)} %get-tuple-element.70), channel_id=1, source_target_pairs={{0,96},{8,104},{16,112},{24,120},{32,64},{40,72},{48,80},{56,88},{... | collective-permute-start | bytes 417800 | tf_op jit(solution)/shard_map/ppermute | solution.py:31
  (71 shorter events, 28.1 us)
Async XLA Ops:
  1.1 6.9 %collective-permute-start.2 = (bf16[128,256]{1,0:T(8,128)(2,1)S(1)}, bf16[128,256]{1,0:T(8,128)(2,1)S(1)}, u32[]{:S(2)}, u32[]{:S(2)}) collective-permute-start(bf16[128,256]{1,0:T(8,128)(2,1)S(1)} %bitcast.38), channel_id=1, source_target_pairs={{0,8},{8,16},{16,24},{24,0},{32,40},{40,48},{48,56},{56,32},{64,72... | collective-permute-start | bytes 196616 | tf_op jit(solution)/shard_map/ppermute | solution.py:52
  3.2 5.7 %collective-permute-start = (bf16[128,256]{1,0:T(8,128)(2,1)S(1)}, bf16[128,256]{1,0:T(8,128)(2,1)S(1)}, u32[]{:S(2)}, u32[]{:S(2)}) collective-permute-start(bf16[128,256]{1,0:T(8,128)(2,1)S(1)} %bitcast.39), channel_id=1, source_target_pairs={{0,24},{8,0},{16,8},{24,16},{32,56},{40,32},{48,40},{56,48},{64,88... | collective-permute-start | bytes 196616 | tf_op jit(solution)/shard_map/ppermute | solution.py:52
  3.5 6.6 %collective-permute-start.1 = (bf16[128,256]{1,0:T(8,128)(2,1)S(1)}, bf16[128,256]{1,0:T(8,128)(2,1)S(1)}, u32[]{:S(2)}, u32[]{:S(2)}) collective-permute-start(bf16[128,256]{1,0:T(8,128)(2,1)S(1)} %bitcast.40), channel_id=1, source_target_pairs={{0,16},{8,24},{16,0},{24,8},{32,48},{40,56},{48,32},{56,40},{64,80... | collective-permute-start | bytes 196616 | tf_op jit(solution)/shard_map/ppermute | solution.py:52
  5.0 25.2 %collective-permute-start.4 = (bf16[256,1792]{1,0:T(8,128)(2,1)}, bf16[256,1792]{1,0:T(8,128)(2,1)S(1)}, u32[]{:S(2)}, u32[]{:S(2)}) collective-permute-start(bf16[256,1792]{1,0:T(8,128)(2,1)} %refs_0_.15), channel_id=1, source_target_pairs={{0,8},{8,16},{16,24},{24,0},{32,40},{40,48},{48,56},{56,32},{64,72... | collective-permute-start | bytes 2752520 | tf_op jit(solution)/shard_map/ppermute | solution.py:52
  7.0 23.3 %collective-permute-start.3 = (bf16[256,1792]{1,0:T(8,128)(2,1)}, bf16[256,1792]{1,0:T(8,128)(2,1)S(1)}, u32[]{:S(2)}, u32[]{:S(2)}) collective-permute-start(bf16[256,1792]{1,0:T(8,128)(2,1)} %refs_0_.15), channel_id=1, source_target_pairs={{0,24},{8,0},{16,8},{24,16},{32,56},{40,32},{48,40},{56,48},{64,88... | collective-permute-start | bytes 2752520 | tf_op jit(solution)/shard_map/ppermute | solution.py:52
  10.1 12.4 %collective-permute-start.9 = (bf16[4,128,256]{2,1,0:T(8,128)(2,1)S(1)}, bf16[4,128,256]{2,1,0:T(8,128)(2,1)S(1)}, u32[]{:S(2)}, u32[]{:S(2)}) collective-permute-start(bf16[4,128,256]{2,1,0:T(8,128)(2,1)S(1)} %pad_maximum_fusion.1), channel_id=1, source_target_pairs={{0,2},{1,3},{2,4},{3,5},{4,6},{5,7},{6,0},{7,1},{8,10},{9,11},{10,... | collective-permute-start | bytes 786440 | tf_op jit(solution)/shard_map/ppermute | solution.py:56
  13.4 14.3 %collective-permute-start.8 = (bf16[4,128,256]{2,1,0:T(8,128)(2,1)S(1)}, bf16[4,128,256]{2,1,0:T(8,128)(2,1)S(1)}, u32[]{:S(2)}, u32[]{:S(2)}) collective-permute-start(bf16[4,128,256]{2,1,0:T(8,128)(2,1)S(1)} %pad_maximum_fusion.1), channel_id=1, source_target_pairs={{0,6},{1,7},{2,0},{3,1},{4,2},{5,3},{6,4},{7,5},{8,14},{9,15},{10,... | collective-permute-start | bytes 786440 | tf_op jit(solution)/shard_map/ppermute | solution.py:56
  16.5 15.4 %collective-permute-start.7 = (bf16[4,128,256]{2,1,0:T(8,128)(2,1)S(1)}, bf16[4,128,256]{2,1,0:T(8,128)(2,1)S(1)}, u32[]{:S(2)}, u32[]{:S(2)}) collective-permute-start(bf16[4,128,256]{2,1,0:T(8,128)(2,1)S(1)} %pad_maximum_fusion.1), channel_id=1, source_target_pairs={{0,1},{1,0},{2,3},{3,2},{4,5},{5,4},{6,7},{7,6},{8,9},{9,8},{10,11... | collective-permute-start | bytes 786440 | tf_op jit(solution)/shard_map/ppermute | solution.py:60
  22.5 10.5 %collective-permute-start.11 = (bf16[2,128,256]{2,1,0:T(8,128)(2,1)S(1)}, bf16[2,128,256]{2,1,0:T(8,128)(2,1)S(1)}, u32[]{:S(2)}, u32[]{:S(2)}) collective-permute-start(bf16[2,128,256]{2,1,0:T(8,128)(2,1)S(1)} %slice_bitcast_fusion.1), channel_id=1, source_target_pairs={{0,2},{1,3},{2,4},{3,5},{4,6},{5,7},{6,0},{7,1},{8,10},{9,11},{10,... | collective-permute-start | bytes 393224 | tf_op jit(solution)/shard_map/ppermute | solution.py:56
  27.8 8.6 %collective-permute-start.12 = (bf16[2,128,256]{2,1,0:T(8,128)(2,1)S(1)}, bf16[2,128,256]{2,1,0:T(8,128)(2,1)S(1)}, u32[]{:S(2)}, u32[]{:S(2)}) collective-permute-start(bf16[2,128,256]{2,1,0:T(8,128)(2,1)S(1)} %slice_bitcast_fusion), channel_id=1, source_target_pairs={{0,6},{1,7},{2,0},{3,1},{4,2},{5,3},{6,4},{7,5},{8,14},{9,15},{10,... | collective-permute-start | bytes 393224 | tf_op jit(solution)/shard_map/ppermute | solution.py:56
  30.2 15.7 %collective-permute-start.10 = (bf16[2,4,128,256]{3,2,1,0:T(8,128)(2,1)S(1)}, bf16[2,4,128,256]{3,2,1,0:T(8,128)(2,1)S(1)}, u32[]{:S(2)}, u32[]{:S(2)}) collective-permute-start(bf16[2,4,128,256]{3,2,1,0:T(8,128)(2,1)S(1)} %pad_maximum_fusion), channel_id=1, source_target_pairs={{0,1},{1,0},{2,3},{3,2},{4,5},{5,4},{6,7},{7,6},{8,9},{9,8},{10,11... | collective-permute-start | bytes 1572872 | tf_op jit(solution)/shard_map/ppermute | solution.py:60
  30.3 13.0 %collective-permute-start.5 = (bf16[128,1792]{1,0:T(8,128)(2,1)S(1)}, bf16[128,1792]{1,0:T(8,128)(2,1)S(1)}, u32[]{:S(2)}, u32[]{:S(2)}) collective-permute-start(bf16[128,1792]{1,0:T(8,128)(2,1)S(1)} %slice.24), channel_id=1, source_target_pairs={{0,8},{8,16},{16,24},{24,0},{32,40},{40,48},{48,56},{56,32},{64,72... | collective-permute-start | bytes 1376264 | tf_op jit(solution)/shard_map/ppermute | solution.py:52
  31.9 13.9 %collective-permute-start.6 = (bf16[128,1792]{1,0:T(8,128)(2,1)S(1)}, bf16[128,1792]{1,0:T(8,128)(2,1)S(1)}, u32[]{:S(2)}, u32[]{:S(2)}) collective-permute-start(bf16[128,1792]{1,0:T(8,128)(2,1)S(1)} %slice.25), channel_id=1, source_target_pairs={{0,24},{8,0},{16,8},{24,16},{32,56},{40,32},{48,40},{56,48},{64,88... | collective-permute-start | bytes 1376264 | tf_op jit(solution)/shard_map/ppermute | solution.py:52
  49.8 16.7 %collective-permute-start.14 = (bf16[2,1040,128]{2,1,0:T(8,128)(2,1)S(1)}, bf16[2,1040,128]{2,1,0:T(8,128)(2,1)S(1)}, u32[]{:S(2)}, u32[]{:S(2)}) collective-permute-start(bf16[2,1040,128]{2,1,0:T(8,128)(2,1)S(1)} %sent_sums.4), channel_id=1, source_target_pairs={{0,32},{8,40},{16,48},{24,56},{32,0},{40,8},{48,16},{56,24},{64,96... | collective-permute-start | bytes 1597448 | tf_op jit(solution)/shard_map/ppermute | solution.py:31
  53.9 17.1 %collective-permute-start.15 = (bf16[2,1040,128]{2,1,0:T(8,128)(2,1)S(1)}, bf16[2,1040,128]{2,1,0:T(8,128)(2,1)S(1)}, u32[]{:S(2)}, u32[]{:S(2)}) collective-permute-start(bf16[2,1040,128]{2,1,0:T(8,128)(2,1)S(1)} %sent_sums.5), channel_id=1, source_target_pairs={{0,96},{8,104},{16,112},{24,120},{32,64},{40,72},{48,80},{56,88},{... | collective-permute-start | bytes 1597448 | tf_op jit(solution)/shard_map/ppermute | solution.py:31
  58.4 15.6 %collective-permute-start.16 = (bf16[2,1040,128]{2,1,0:T(8,128)(2,1)S(1)}, bf16[2,1040,128]{2,1,0:T(8,128)(2,1)S(1)}, u32[]{:S(2)}, u32[]{:S(2)}) collective-permute-start(bf16[2,1040,128]{2,1,0:T(8,128)(2,1)S(1)} %sent_sums.6), channel_id=1, source_target_pairs={{0,128},{8,136},{16,144},{24,152},{32,160},{40,168},{48,176},{56,1... | collective-permute-start | bytes 1597448 | tf_op jit(solution)/shard_map/ppermute | solution.py:31
  61.4 15.0 %collective-permute-start.17 = (bf16[1,1040,128]{2,1,0:T(8,128)(2,1)S(1)}, bf16[1,1040,128]{2,1,0:T(8,128)(2,1)S(1)}, u32[]{:S(2)}, u32[]{:S(2)}) collective-permute-start(bf16[1,1040,128]{2,1,0:T(8,128)(2,1)S(1)} %sent_sums.7), channel_id=1, source_target_pairs={{0,32},{8,40},{16,48},{24,56},{32,0},{40,8},{48,16},{56,24},{64,96... | collective-permute-start | bytes 798728 | tf_op jit(solution)/shard_map/ppermute | solution.py:31
  67.5 11.8 %collective-permute-start.18 = (bf16[2,528,128]{2,1,0:T(8,128)(2,1)S(1)}, bf16[2,528,128]{2,1,0:T(8,128)(2,1)S(1)}, u32[]{:S(2)}, u32[]{:S(2)}) collective-permute-start(bf16[2,528,128]{2,1,0:T(8,128)(2,1)S(1)} %get-tuple-element.58), channel_id=1, source_target_pairs={{0,96},{8,104},{16,112},{24,120},{32,64},{40,72},{48,80},{56,88},{... | collective-permute-start | bytes 811016 | tf_op jit(solution)/shard_map/ppermute | solution.py:31
  72.0 9.5 %collective-permute-start.19 = (bf16[2,528,128]{2,1,0:T(8,128)(2,1)S(1)}, bf16[2,528,128]{2,1,0:T(8,128)(2,1)S(1)}, u32[]{:S(2)}, u32[]{:S(2)}) collective-permute-start(bf16[2,528,128]{2,1,0:T(8,128)(2,1)S(1)} %get-tuple-element.61), channel_id=1, source_target_pairs={{0,32},{8,40},{16,48},{24,56},{32,0},{40,8},{48,16},{56,24},{64,96... | collective-permute-start | bytes 811016 | tf_op jit(solution)/shard_map/ppermute | solution.py:31
  75.0 9.6 %collective-permute-start.20 = (bf16[2,528,128]{2,1,0:T(8,128)(2,1)S(1)}, bf16[2,528,128]{2,1,0:T(8,128)(2,1)S(1)}, u32[]{:S(2)}, u32[]{:S(2)}) collective-permute-start(bf16[2,528,128]{2,1,0:T(8,128)(2,1)S(1)} %get-tuple-element.64), channel_id=1, source_target_pairs={{0,32},{8,40},{16,48},{24,56},{32,0},{40,8},{48,16},{56,24},{64,96... | collective-permute-start | bytes 811016 | tf_op jit(solution)/shard_map/ppermute | solution.py:31
  77.2 10.6 %collective-permute-start.21 = (bf16[1,528,128]{2,1,0:T(8,128)(2,1)S(1)}, bf16[1,528,128]{2,1,0:T(8,128)(2,1)S(1)}, u32[]{:S(2)}, u32[]{:S(2)}) collective-permute-start(bf16[1,528,128]{2,1,0:T(8,128)(2,1)S(1)} %get-tuple-element.67), channel_id=1, source_target_pairs={{0,96},{8,104},{16,112},{24,120},{32,64},{40,72},{48,80},{56,88},{... | collective-permute-start | bytes 405512 | tf_op jit(solution)/shard_map/ppermute | solution.py:31
  80.0 9.0 %collective-permute-start.25 = (bf16[2,272,128]{2,1,0:T(8,128)(2,1)S(1)}, bf16[2,272,128]{2,1,0:T(8,128)(2,1)S(1)}, u32[]{:S(2)}, u32[]{:S(2)}) collective-permute-start(bf16[2,272,128]{2,1,0:T(8,128)(2,1)S(1)} %get-tuple-element.72), channel_id=1, source_target_pairs={{0,128},{8,136},{16,144},{24,152},{32,160},{40,168},{48,176},{56,1... | collective-permute-start | bytes 417800 | tf_op jit(solution)/shard_map/ppermute | solution.py:31
  82.3 7.7 %collective-permute-start.24 = (bf16[2,272,128]{2,1,0:T(8,128)(2,1)S(1)}, bf16[2,272,128]{2,1,0:T(8,128)(2,1)S(1)}, u32[]{:S(2)}, u32[]{:S(2)}) collective-permute-start(bf16[2,272,128]{2,1,0:T(8,128)(2,1)S(1)} %get-tuple-element.71), channel_id=1, source_target_pairs={{0,128},{8,136},{16,144},{24,152},{32,160},{40,168},{48,176},{56,1... | collective-permute-start | bytes 417800 | tf_op jit(solution)/shard_map/ppermute | solution.py:31
  85.4 6.4 %collective-permute-start.23 = (bf16[2,272,128]{2,1,0:T(8,128)(2,1)S(1)}, bf16[2,272,128]{2,1,0:T(8,128)(2,1)S(1)}, u32[]{:S(2)}, u32[]{:S(2)}) collective-permute-start(bf16[2,272,128]{2,1,0:T(8,128)(2,1)S(1)} %get-tuple-element.70), channel_id=1, source_target_pairs={{0,96},{8,104},{16,112},{24,120},{32,64},{40,72},{48,80},{56,88},{... | collective-permute-start | bytes 417800 | tf_op jit(solution)/shard_map/ppermute | solution.py:31
  (3 other events, 21.5 us)
